TPU v7x, 512 devices: a whole 4x8x8 slice. The times are simulated.
512 devices in a mesh: replica: 4 (over z_hi), row: 16 (over z_lo, y), col: 8 (over x, core).
Axes of the slice: x: 4, y: 8, z: 8 (z_hi: 4, z_lo: 2; z = z_hi * 2 + z_lo), core: 2. Of those that a mesh axis runs over, the one named last changes fastest.
Arguments:
- hidden: bfloat16 [4, 1408, 14336], P('replica', 'col', 'row'), may hold values from -6 to 6
- cotangent: bfloat16 [4, 1408, 4096], P('replica', 'row', 'col'), may hold values from -6 to 6
- weight: bfloat16 [4, 14336, 4096], P('replica', 'row', 'col'), may hold values from -6 to 6
- prev_weight: bfloat16 [4, 14336, 4096], P('replica', 'row', 'col'), may hold values from -6 to 6
- prev_grad: bfloat16 [4, 14336, 4096], P('replica', 'row', 'col'), may hold values from -3 to 3
Outputs:
- output: bfloat16 [4, 1408, 4096], P('replica', 'row', 'col')
- hidden_grad: bfloat16 [4, 1408, 14336], P('replica', 'col', 'row')
- new_weight: bfloat16 [4, 14336, 4096], P('replica', 'row', 'col')
All inputs are finite; a program needn't handle non-finite values.
Results may differ from a plain program's by a relative error of at most 0.017.
Values may be sent and summed in bfloat16 or wider, within the bound.
No kernel may reach another device: no remote copies, remote signals or barrier semaphores. Data moves between devices by JAX's collectives and lax.ppermute only.
A program may use at most 64 MiB of HBM per device.

v0:
```python
import jax
import jax.numpy as jnp
from jax import lax
from jax.sharding import Mesh
from jax.sharding import PartitionSpec as P

FF = 14336
ROW = ("row_0", "row_1")


def shifted(array, axis, by):
    peers = lax.axis_size(axis)
    return lax.ppermute(array, axis, [(i, (i + by) % peers) for i in range(peers)])


def joined_along(parts, dim):
    parts = jnp.moveaxis(parts, 0, dim)
    shape = parts.shape
    return parts.reshape(*shape[:dim], shape[dim] * shape[dim + 1], *shape[dim + 2 :])


def copy_for_each(array, axis):
    peers = lax.axis_size(axis)
    return lax.all_to_all(
        jnp.broadcast_to(array[None], (peers, *array.shape)), axis, 0, 0, tiled=True
    )


def gathered_copies(array, axis, dim):
    return joined_along(copy_for_each(array, axis), dim)


def own_block(parts, axes, sequence):
    inside = parts.shape[1:]
    parts = parts.reshape(*(lax.axis_size(a) for a in axes), *inside)
    parts = jnp.moveaxis(parts, sequence, range(len(axes))).reshape(-1, *inside)
    for k in sequence:
        parts = lax.psum_scatter(parts, axes[k], scatter_dimension=0, tiled=True)
    return parts[0]


def in_blocks(array, dim, peers):
    shape = array.shape
    parts = array.reshape(*shape[:dim], peers, shape[dim] // peers, *shape[dim + 1 :])
    return jnp.moveaxis(parts, dim, 0)


def summed_rows(array, axes, sequence, dim):
    peers = lax.axis_size(axes)
    return own_block(in_blocks(array, dim, peers), axes, sequence)


def summed_on_arrival(array, axis, dim):
    parts = in_blocks(array, dim, lax.axis_size(axis))
    arrived = lax.all_to_all(parts, axis, split_axis=0, concat_axis=0, tiled=True)
    return arrived.astype(jnp.float32).sum(axis=0)


def neighbours(blend):
    left = shifted(blend, "replica", 1)
    right = shifted(blend, "replica", -1)
    return (left.astype(jnp.float32), right.astype(jnp.float32))


def on_device(hidden, cotangent, weight, prev_weight, prev_grad):
    scale = FF ** (-0.5)
    blend_low = (weight[0].astype(jnp.float32) - 0.5 * prev_weight[0].astype(jnp.float32)).astype(
        jnp.bfloat16
    )
    gathered = gathered_copies(hidden[0], "col", 0)
    upstream = gathered_copies(cotangent[0], ROW, 0)
    matrix = weight[0]
    partial_value = jnp.dot(gathered, matrix, preferred_element_type=jnp.float32) * scale
    output = (
        summed_rows(partial_value.astype(jnp.bfloat16), ROW, (1, 0), 0)
        .astype(jnp.float32)
        .astype(jnp.bfloat16)
    )
    term = (
        lax.dot_general(
            upstream, matrix, (((1,), (1,)), ((), ())), preferred_element_type=jnp.float32
        )
        * scale
    )
    hidden_grad = summed_on_arrival(term.astype(jnp.bfloat16), "col", 0)
    grad = (
        lax.dot_general(
            gathered, upstream, (((0,), (0,)), ((), ())), preferred_element_type=jnp.float32
        )
        * scale
    )
    left, right = neighbours(blend_low)
    blend = blend_low.astype(jnp.float32)
    fresh = blend + (left + blend + right) / 3.0 - 0.5 * (grad - prev_grad[0].astype(jnp.float32))
    return (output[None], hidden_grad.astype(jnp.bfloat16)[None], fresh.astype(jnp.bfloat16)[None])


def solution(mesh):
    torus = Mesh(
        mesh.devices.reshape(mesh.shape["replica"], 2, 8, mesh.shape["col"]),
        ("replica", "row_0", "row_1", "col"),
    )
    return jax.shard_map(
        on_device,
        mesh=torus,
        in_specs=(
            P("replica", "col", ROW),
            P("replica", ROW, "col"),
            P("replica", ROW, "col"),
            P("replica", ROW, "col"),
            P("replica", ROW, "col"),
        ),
        out_specs=(P("replica", ROW, "col"), P("replica", "col", ROW), P("replica", ROW, "col")),
        check_vma=False,
    )
```

profile of v0, /device:TPU:1, one launch (start us, length us, event | category | flops | bytes accessed | tf_op | source)
XLA Modules:
  0.0 177.0 jit_solution(11022181734125833299)
XLA Ops:
  7.2 1.2 broadcast_in_dim.22
  8.3 0.0 copy-start.2
  8.3 40.7 %all_to_all.15 = bf16[8,176,896]{2,1,0:T(8,128)(2,1)S(1)} all-to-all(bf16[8,176,896]{2,1,0:T(8,128)(2,1)S(1)} %broadcast_in_dim.22), channel_id=1, replica_groups=mesh['replica'=4,'row_0'=2,'row_1'=8,'col'=8] {'col'}, dimensions={0} | all-to-all | bytes 5046272 | tf_op jit(solution)/shard_map/all_to_all | solution.py:24
  49.0 0.0 copy-start
  49.0 0.0 copy-done.2
  49.0 0.0 copy-start.1
  49.0 1.2 broadcast_in_dim.24
  50.2 5.1 %all-to-all-start.1 = ((bf16[16,88,512]{2,1,0:T(8,128)(2,1)}), bf16[16,88,512]{2,1,0:T(8,128)(2,1)}, u32[]{:S(2)}, u32[]{:S(2)}) async-start(bf16[16,88,512]{2,1,0:T(8,128)(2,1)} %broadcast_in_dim.24), calls=%async_computation.3 | async-start | bytes 2883584 | tf_op jit(solution)/shard_map/all_to_all | solution.py:24
  55.3 0.0 reduce-scatter.3.cloned.1.call-start
  55.3 0.0 copy-done
  55.3 0.0 copy-done.1
  55.3 1.7 fusion
  57.0 1.2 copy.8
  58.2 0.0 reduce-scatter.3.cloned.1.call-update
  58.3 34.2 %all-to-all-done.1 = bf16[16,88,512]{2,1,0:T(8,128)(2,1)} async-done(((bf16[16,88,512]{2,1,0:T(8,128)(2,1)}), bf16[16,88,512]{2,1,0:T(8,128)(2,1)}, u32[]{:S(2)}, u32[]{:S(2)}) %all-to-all-start.1) | async-done | bytes 1441824 | tf_op jit(solution)/shard_map/all_to_all | solution.py:24
  92.5 4.6 %multiply_convert_fusion = bf16[1408,896]{1,0:T(8,128)(2,1)} fusion(bf16[1408,512]{1,0:T(8,128)(2,1)} %bitcast.7, bf16[1,896,512]{2,1,0:T(8,128)(2,1)S(1)} %copy-done.1), kind=kOutput, calls=%fused_computation | convolution fusion | flops 1294368768 | bytes 4882432 | tf_op jit(solution)/shard_map/dot_general | solution.py:80
  97.1 8.5 %all-to-all-start.2 = ((bf16[8,176,896]{2,1,0:T(8,128)(2,1)}), bf16[8,176,896]{2,1,0:T(8,128)(2,1)S(1)}, u32[]{:S(2)}, u32[]{:S(2)}) async-start(bf16[8,176,896]{2,1,0:T(8,128)(2,1)} %bitcast.32), calls=%async_computation.4 | async-start | bytes 5046272 | tf_op jit(solution)/shard_map/all_to_all | solution.py:55
  105.5 0.0 reduce-scatter.5.cloned.1.call-start
  105.5 2.4 %fusion.6 = bf16[896,512]{1,0:T(8,128)(2,1)} fusion(bf16[1,896,512]{2,1,0:T(8,128)(2,1)} %param.8, bf16[1,896,512]{2,1,0:T(8,128)(2,1)S(1)} %copy-done.1), kind=kLoop, calls=%fused_computation.12 | loop fusion | flops 2293760 | bytes 2752512 | tf_op jit(solution)/shard_map/convert_element_type | solution.py:67
  107.9 6.9 %collective-permute-start = (bf16[896,512]{1,0:T(8,128)(2,1)}, bf16[896,512]{1,0:T(8,128)(2,1)S(1)}, u32[]{:S(2)}, u32[]{:S(2)}) collective-permute-start(bf16[896,512]{1,0:T(8,128)(2,1)} %fusion.6), channel_id=1, source_target_pairs={{0,128},{128,256},{256,384},{384,0},{1,129},{129,257},{257,385},{3... | collective-permute-start | bytes 2752520 | tf_op jit(solution)/shard_map/ppermute | solution.py:13
  114.9 7.8 %collective-permute-start.1 = (bf16[896,512]{1,0:T(8,128)(2,1)}, bf16[896,512]{1,0:T(8,128)(2,1)}, u32[]{:S(2)}, u32[]{:S(2)}) collective-permute-start(bf16[896,512]{1,0:T(8,128)(2,1)} %fusion.6), channel_id=1, source_target_pairs={{0,384},{128,0},{256,128},{384,256},{1,385},{129,1},{257,129},{385... | collective-permute-start | bytes 2752520 | tf_op jit(solution)/shard_map/ppermute | solution.py:13
  122.6 0.0 reduce-scatter.3.cloned.1.call-done
  122.7 0.0 reduce-scatter.5.cloned.1.call-update
  122.7 40.4 %collective-permute-done = bf16[896,512]{1,0:T(8,128)(2,1)S(1)} collective-permute-done((bf16[896,512]{1,0:T(8,128)(2,1)}, bf16[896,512]{1,0:T(8,128)(2,1)S(1)}, u32[]{:S(2)}, u32[]{:S(2)}) %collective-permute-start) | collective-permute-done | bytes 917536 | tf_op jit(solution)/shard_map/ppermute | solution.py:13
  163.1 0.0 collective-permute-done.1
  163.1 5.9 %fusion.7 = bf16[1,896,512]{2,1,0:T(8,128)(2,1)} fusion(bf16[1408,896]{1,0:T(8,128)(2,1)} %bitcast.31, bf16[1408,512]{1,0:T(8,128)(2,1)} %bitcast.7, bf16[896,512]{1,0:T(8,128)(2,1)} %collective-permute-done.1, bf16[896,512]{1,0:T(8,128)(2,1)S(1)} %collective-permute-done, bf16[896,512]{1,0:T(8,128)(2,1)} %fusion.6, bf16[1,896,512]{2,1,0:T(8,128)(2,1)} %param.9), kind=kOutput, calls=%fused_computation.13 | convolution fusion | flops 1297809408 | bytes 8552448 | tf_op jit(solution)/shard_map/dot_general | solution.py:87
  169.0 0.0 all-to-all-done.2
  169.0 1.1 reduce_sum.12
  170.1 0.0 reduce-scatter.5.cloned.1.call-done
Async XLA Ops:
  8.3 40.7 %copy-start.2 = (bf16[1,88,512]{2,1,0:T(8,128)(2,1)S(1)}, bf16[1,88,512]{2,1,0:T(8,128)(2,1)}, u32[]{:S(2)}) copy-start(bf16[1,88,512]{2,1,0:T(8,128)(2,1)} %param.6) | copy-start | bytes 270340
  49.0 6.3 %copy-start = (bf16[8,176,896]{2,1,0:T(8,128)(2,1)}, bf16[8,176,896]{2,1,0:T(8,128)(2,1)S(1)}, u32[]{:S(2)}) copy-start(bf16[8,176,896]{2,1,0:T(8,128)(2,1)S(1)} %all_to_all.15) | copy-start | bytes 7569412
  49.0 6.3 %copy-start.1 = (bf16[1,896,512]{2,1,0:T(8,128)(2,1)S(1)}, bf16[1,896,512]{2,1,0:T(8,128)(2,1)}, u32[]{:S(2)}) copy-start(bf16[1,896,512]{2,1,0:T(8,128)(2,1)} %param.7) | copy-start | bytes 2752516
  50.2 42.3 %all-to-all-start.1 = ((bf16[16,88,512]{2,1,0:T(8,128)(2,1)}), bf16[16,88,512]{2,1,0:T(8,128)(2,1)}, u32[]{:S(2)}, u32[]{:S(2)}) async-start(bf16[16,88,512]{2,1,0:T(8,128)(2,1)} %broadcast_in_dim.24), calls=%async_computation.3 | async-start | bytes 2883584 | tf_op jit(solution)/shard_map/all_to_all | solution.py:24
  55.3 67.4 %reduce-scatter.3.cloned.1.call-start = ((), (), s32[]{:S(2)}) async-start(), calls=%async_computation.5 | async-start | bytes 1622016 | tf_op jit(solution)/shard_map/reduce_scatter | solution.py:38
  97.1 71.9 %all-to-all-start.2 = ((bf16[8,176,896]{2,1,0:T(8,128)(2,1)}), bf16[8,176,896]{2,1,0:T(8,128)(2,1)S(1)}, u32[]{:S(2)}, u32[]{:S(2)}) async-start(bf16[8,176,896]{2,1,0:T(8,128)(2,1)} %bitcast.32), calls=%async_computation.4 | async-start | bytes 5046272 | tf_op jit(solution)/shard_map/all_to_all | solution.py:55
  105.5 64.6 %reduce-scatter.5.cloned.1.call-start = ((), (), s32[]{:S(2)}) async-start(), calls=%async_computation.6 | async-start | bytes 270336 | tf_op jit(solution)/shard_map/reduce_scatter | solution.py:38
  107.9 55.2 %collective-permute-start = (bf16[896,512]{1,0:T(8,128)(2,1)}, bf16[896,512]{1,0:T(8,128)(2,1)S(1)}, u32[]{:S(2)}, u32[]{:S(2)}) collective-permute-start(bf16[896,512]{1,0:T(8,128)(2,1)} %fusion.6), channel_id=1, source_target_pairs={{0,128},{128,256},{256,384},{384,0},{1,129},{129,257},{257,385},{3... | collective-permute-start | bytes 2752520 | tf_op jit(solution)/shard_map/ppermute | solution.py:13
  114.9 48.2 %collective-permute-start.1 = (bf16[896,512]{1,0:T(8,128)(2,1)}, bf16[896,512]{1,0:T(8,128)(2,1)}, u32[]{:S(2)}, u32[]{:S(2)}) collective-permute-start(bf16[896,512]{1,0:T(8,128)(2,1)} %fusion.6), channel_id=1, source_target_pairs={{0,384},{128,0},{256,128},{384,256},{1,385},{129,1},{257,129},{385... | collective-permute-start | bytes 2752520 | tf_op jit(solution)/shard_map/ppermute | solution.py:13
Sparse Core Ops, SparseCore 0:
  59.0 48.5 reduce-scatter.2
  122.8 35.5 reduce-scatter.4
where the time goes:
time: 177 us
  waiting for transfers between devices  74.7 us (42%)
  blocking collectives  40.7 us (23%)
  starting transfers between devices  28.3 us (16%)
  between operations  14.1 us (8%)
  matrix products  12.1 us (7%)
  local copies, waits for them, and re-layouts  3.62 us (2%)
  other arithmetic  3.52 us (2%)
    all_to_all x1, blocking collectives, copy_for_each(): lax.all_to_all(jnp.broadcast_to(array[None], (peers, *array.shape)), axis...  40.7 us
    ppermute x2, waiting for transfers between devices, shifted(): lax.ppermute(array, axis, [(i, (i + by) % peers) for i in range(peers)])  40.4 us
    all_to_all x1, waiting for transfers between devices, copy_for_each(): lax.all_to_all(jnp.broadcast_to(array[None], (peers, *array.shape)), axis...  34.2 us
    ppermute x2, starting transfers between devices, shifted(): lax.ppermute(array, axis, [(i, (i + by) % peers) for i in range(peers)])  14.7 us
    all_to_all x1, starting transfers between devices, summed_on_arrival(): lax.all_to_all(parts, axis, split_axis=0, concat_axis=0, tiled=True)  8.46 us
    dot_general x1, matrix products, on_device(): lax.dot_general(gathered, upstream, (((0,), (0,)), ((), ())), preferred_e...  5.89 us
    all_to_all x1, starting transfers between devices, copy_for_each(): lax.all_to_all(jnp.broadcast_to(array[None], (peers, *array.shape)), axis...  5.07 us
    dot_general x1, matrix products, on_device(): lax.dot_general(upstream, matrix, (((1,), (1,)), ((), ())), preferred_ele...  4.56 us
  transfers between devices with their start and end apart: 6, of which 2 were waited for; matrix products, arithmetic and copies ran while one was open for 10% of the time, Pallas kernels for 0%

commit v1 on v0

v1 whole, which is shorter than its diff:
```python
import jax
import jax.numpy as jnp
from jax import lax
from jax.experimental import pallas as pl
from jax.experimental.pallas import tpu as pltpu
from jax.sharding import Mesh
from jax.sharding import PartitionSpec as P

FF = 14336
SCALE = FF ** (-0.5)
ROW = ("z", "y")
COL = ("x", "c")
F32 = jnp.float32
BF16 = jnp.bfloat16
PARAMS = pltpu.CompilerParams(vmem_limit_bytes=16 * 2**20)
N_X = 4


def shifted(array, axis, by):
    peers = lax.axis_size(axis)
    return lax.ppermute(array, axis, [(i, (i + by) % peers) for i in range(peers)])


def exchanged(parts, axis):
    return lax.all_to_all(parts, axis, 0, 0, tiled=False)


def dot(a, b, ca, cb):
    return lax.dot_general(a, b, (((ca,), (cb,)), ((), ())), preferred_element_type=F32)


def column(d, other):
    x, c = lax.axis_index("x"), lax.axis_index("c")
    return (x + d) % N_X * 2 + (1 - c if other else c)


def fan_kernel(u, u_z, out):
    for y in range(out.shape[0]):
        out[y, 0] = u[...]
        out[y, 1] = u_z[...]


def fan(u, u_z):
    return pl.pallas_call(
        fan_kernel,
        out_shape=jax.ShapeDtypeStruct((2 * N_X, 2, *u.shape), u.dtype),
        compiler_params=PARAMS,
        name="fan",
    )(u, u_z)


def forward_kernel(*refs):
    blocks, (w, out) = refs[:-2], refs[-2:]
    rows = out.shape[1]
    for k, block in enumerate(blocks):
        at = column(k % N_X, k >= N_X)
        term = dot(block[...], w[...], 1, 0) * SCALE
        out[2 * at] = term[:rows].astype(BF16)
        out[2 * at + 1] = term[rows:].astype(BF16)


def forward(blocks, w, rows):
    return pl.pallas_call(
        forward_kernel,
        out_shape=jax.ShapeDtypeStruct((4 * N_X, rows, w.shape[1]), BF16),
        compiler_params=PARAMS,
        name="forward",
    )(*blocks, w)


def backward_kernel(u, w, send, keep, ordered):
    for other in (1, 0):
        for d in range(N_X):
            at = column(d, other)
            y, far = 2 * at % (2 * N_X), (at // N_X + lax.axis_index("z")) % 2
            pair = [u[y + j, far].astype(F32) for j in range(2)]
            both = jnp.concatenate(pair).astype(BF16)
            ordered[other * N_X + d] = both
            term = dot(both, w[...], 1, 1) * SCALE
            (send if other else keep)[d] = term.astype(BF16)


def backward(u, w):
    rows, feats = u.shape[2:]
    half = jax.ShapeDtypeStruct((N_X, 2 * rows, w.shape[0]), BF16)
    return pl.pallas_call(
        backward_kernel,
        out_shape=[half, half, jax.ShapeDtypeStruct((2 * N_X, 2 * rows, feats), BF16)],
        compiler_params=PARAMS,
        name="backward",
    )(u, w)


def step_kernel(*refs):
    blocks, (u, blend, prev, out) = refs[:-4], refs[-4:]
    h = jnp.concatenate([block[...] for block in blocks])
    grad = dot(h, u[...], 0, 0)
    out[...] = blend[...].astype(F32) * (4.0 / 3.0) - 0.5 * (
        grad * SCALE - prev[...].astype(F32)
    )


def local_step(blocks, u, blend, prev):
    units, feats = blend.shape
    h_spec = pl.BlockSpec((blocks[0].shape[0], 128), lambda i: (0, i))
    w_spec = pl.BlockSpec((128, feats), lambda i: (i, 0))
    return pl.pallas_call(
        step_kernel,
        grid=(units // 128,),
        out_shape=jax.ShapeDtypeStruct((units, feats), F32),
        in_specs=[h_spec] * len(blocks) + [pl.BlockSpec(u.shape, lambda i: (0, 0)), w_spec, w_spec],
        out_specs=w_spec,
        compiler_params=PARAMS,
        name="step",
    )(*blocks, u, blend, prev)


def on_device(hidden, cotangent, weight, prev_weight, prev_grad):
    tok, units = hidden.shape[1:]
    rows, feats = cotangent.shape[1:]
    h, u, w = hidden[0], cotangent[0], weight[0]

    blend = (w.astype(F32) - 0.5 * prev_weight[0].astype(F32)).astype(BF16)
    cut = units * 3 // 8
    left = [shifted(blend[:cut], "replica", 1), shifted(blend[cut:], "replica", 1)]
    right = [shifted(blend[:cut], "replica", -1), shifted(blend[cut:], "replica", -1)]

    u_all = exchanged(fan(u, shifted(u, "z", 1)), "y")

    blocks = [h, shifted(h, "x", -1), shifted(h, "x", 2), shifted(h, "x", 1)]
    blocks += [shifted(block, "c", 1) for block in blocks]

    o = forward(blocks, w, rows)
    left[0], right[0], o = lax.optimization_barrier((left[0], right[0], o))
    o = exchanged(o, ROW)
    output = o.astype(F32).sum(axis=0).astype(BF16)

    b_send, b_keep, u_rel = backward(u_all, w)
    b = shifted(b_send, "c", 1).astype(F32) + b_keep.astype(F32)
    got = [shifted(b[d].astype(BF16), "x", d) for d in range(1, N_X)]
    left[1], right[1], *got = lax.optimization_barrier((left[1], right[1], *got))
    hidden_grad = b[0] + sum(part.astype(F32) for part in got)

    base = local_step(blocks, u_rel.reshape(2 * N_X * tok, feats), blend, prev_grad[0])
    around = jnp.concatenate([a.astype(F32) + b.astype(F32) for a, b in zip(left, right)])
    fresh = (base + around / 3.0).astype(BF16)
    return output[None], hidden_grad.astype(BF16)[None], fresh[None]


def solution(mesh):
    torus = Mesh(
        mesh.devices.reshape(mesh.shape["replica"], 2, 8, N_X, 2),
        ("replica", "z", "y", "x", "c"),
    )
    return jax.shard_map(
        on_device,
        mesh=torus,
        in_specs=(
            P("replica", COL, ROW),
            P("replica", ROW, COL),
            P("replica", ROW, COL),
            P("replica", ROW, COL),
            P("replica", ROW, COL),
        ),
        out_specs=(P("replica", ROW, COL), P("replica", COL, ROW), P("replica", ROW, COL)),
        check_vma=False,
    )
```

time: 177 us -> 126 us (0.71); the launches traced: 177 us -> 124 us
  waiting for transfers between devices: 74.7 us -> 18.3 us
  starting transfers between devices: 28.3 us -> 75.7 us
  blocking collectives: 40.7 us -> 0 us
  between operations: 14.1 us -> 1.12 us
  matrix products: 12.1 us -> 0 us
  Pallas kernels: 0 us -> 11.2 us
  other arithmetic: 3.52 us -> 11.7 us
  local copies, waits for them, and re-layouts: 3.62 us -> 5.93 us
    all_to_all x1 -> x0, blocking collectives: 40.7 us -> none  [copy_for_each(): lax.all_to_all(jnp.broadcast_to(array[None], (peers, *array.shape)), axis...]
    ppermute x2 -> x16, starting transfers between devices: 14.7 us -> 55.3 us  [shifted(): lax.ppermute(array, axis, [(i, (i + by) % peers) for i in range(peers)])]
    all_to_all x2, waiting for transfers between devices: 34.3 us -> 2.61 us  [exchanged(): return lax.all_to_all(parts, axis, 0, 0, tiled=False)]
    ppermute x2 -> x16, waiting for transfers between devices: 40.4 us -> 15.7 us  [shifted(): lax.ppermute(array, axis, [(i, (i + by) % peers) for i in range(peers)])]
    dot_general x3 -> x0, matrix products: 12.1 us -> none  [the longest x1 5.89 us: on_device(): lax.dot_general(gathered, upstream, (((0,), (0,)), ((), ())), preferred_e...]
    pallas_call x0 -> x4, Pallas kernels: none -> 11.2 us  [the longest x1 4.87 us: local_step(): pl.pallas_call(step_kernel, grid=(units // 128,), out_shape=jax.ShapeDtyp...]
    all_to_all x2, starting transfers between devices: 13.5 us -> 20.4 us  [exchanged(): return lax.all_to_all(parts, axis, 0, 0, tiled=False)]
    add x0 -> x3, other arithmetic: none -> 4.27 us  [the longest x2 2.48 us: on_device(): a.astype(F32) + b.astype(F32)]
  transfers between devices with their start and end apart: 6 -> 18, of which waited for: 2 -> 4; matrix products, arithmetic and copies ran while one was open for 10% -> 7% of each run, Pallas kernels for 0% -> 9%
where the time goes in v1:
time: 126 us; the launch traced here: 124 us
  starting transfers between devices  75.7 us (60%)
  waiting for transfers between devices  18.3 us (15%)
  other arithmetic  11.7 us (9%)
  Pallas kernels  11.2 us (9%)
  local copies, waits for them, and re-layouts  5.93 us (5%)
    ppermute x16, starting transfers between devices, shifted(): lax.ppermute(array, axis, [(i, (i + by) % peers) for i in range(peers)])  55.3 us
    all_to_all x2, starting transfers between devices, exchanged(): return lax.all_to_all(parts, axis, 0, 0, tiled=False)  20.4 us
    ppermute x16, waiting for transfers between devices, shifted(): lax.ppermute(array, axis, [(i, (i + by) % peers) for i in range(peers)])  15.7 us
    pallas_call x1, Pallas kernels, local_step(): pl.pallas_call(step_kernel, grid=(units // 128,), out_shape=jax.ShapeDtyp...  4.87 us
    unnamed x44, local copies, waits for them, and re-layouts  4.1 us
    pallas_call x1, Pallas kernels, forward(): pl.pallas_call(forward_kernel, out_shape=jax.ShapeDtypeStruct((4 * N_X, r...  3.9 us
    broadcast_in_dim x2, other arithmetic, on_device(): return (output[None], hidden_grad.astype(BF16)[None], fresh[None])  3.63 us
    all_to_all x2, waiting for transfers between devices, exchanged(): return lax.all_to_all(parts, axis, 0, 0, tiled=False)  2.61 us
  transfers between devices with their start and end apart: 18, of which 4 were waited for; matrix products, arithmetic and copies ran while one was open for 7% of the time, Pallas kernels for 9%

profile of v1, /device:TPU:1, one launch (start us, length us, event | category | flops | bytes accessed | tf_op | source)
XLA Modules:
  0.0 124.0 jit_solution(8039168910874460935)
XLA Ops:
  0.6 4.8 %collective-permute-start.9 = (bf16[88,512]{1,0:T(8,128)(2,1)}, bf16[88,512]{1,0:T(8,128)(2,1)S(1)}, u32[]{:S(2)}, u32[]{:S(2)}) collective-permute-start(bf16[88,512]{1,0:T(8,128)(2,1)} %bitcast.33), channel_id=1, source_target_pairs={{0,64},{64,0},{1,65},{65,1},{2,66},{66,2},{3,67},{67,3},{4,68},{68... | collective-permute-start | bytes 270344 | tf_op jit(solution)/shard_map/ppermute | solution.py:21
  5.5 2.1 %collective-permute-done.9.u_z = bf16[88,512]{1,0:T(8,128)(2,1)S(1)} collective-permute-done((bf16[88,512]{1,0:T(8,128)(2,1)}, bf16[88,512]{1,0:T(8,128)(2,1)S(1)}, u32[]{:S(2)}, u32[]{:S(2)}) %collective-permute-start.9) | collective-permute-done | bytes 90144 | tf_op jit(solution)/shard_map/ppermute | solution.py:21
  7.6 0.9 copy-done.19
  8.5 0.1 fan.1
  8.6 0.0 copy-start.3
  8.6 1.1 copy-done.3
  9.7 7.4 %all-to-all-start.1 = ((bf16[8,2,88,512]{3,2,1,0:T(8,128)(2,1)}), bf16[8,2,88,512]{3,2,1,0:T(8,128)(2,1)S(1)}, u32[]{:S(2)}, u32[]{:S(2)}) async-start(bf16[8,2,88,512]{3,2,1,0:T(8,128)(2,1)} %copy-done.3), calls=%async_computation.1 | async-start | bytes 2883584 | tf_op jit(solution)/shard_map/all_to_all | solution.py:25
  17.1 4.8 %collective-permute-start.5 = (bf16[176,896]{1,0:T(8,128)(2,1)}, bf16[176,896]{1,0:T(8,128)(2,1)S(1)}, u32[]{:S(2)}, u32[]{:S(2)}) collective-permute-start(bf16[176,896]{1,0:T(8,128)(2,1)} %bitcast.2.refs_0_), channel_id=1, source_target_pairs={{0,1},{1,0},{2,3},{3,2},{4,5},{5,4},{6,7},{7,6},{8,9},{9,8},{10,11... | collective-permute-start | bytes 946184 | tf_op jit(solution)/shard_map/ppermute | solution.py:21
  21.9 1.9 %collective-permute-start.4 = (bf16[176,896]{1,0:T(8,128)(2,1)}, bf16[176,896]{1,0:T(8,128)(2,1)S(1)}, u32[]{:S(2)}, u32[]{:S(2)}) collective-permute-start(bf16[176,896]{1,0:T(8,128)(2,1)} %bitcast.2.refs_0_), channel_id=1, source_target_pairs={{0,2},{2,4},{4,6},{6,0},{1,3},{3,5},{5,7},{7,1},{8,10},{10,12},{12... | collective-permute-start | bytes 946184 | tf_op jit(solution)/shard_map/ppermute | solution.py:21
  23.8 4.2 %collective-permute-start.3 = (bf16[176,896]{1,0:T(8,128)(2,1)}, bf16[176,896]{1,0:T(8,128)(2,1)S(1)}, u32[]{:S(2)}, u32[]{:S(2)}) collective-permute-start(bf16[176,896]{1,0:T(8,128)(2,1)} %bitcast.2.refs_0_), channel_id=1, source_target_pairs={{0,4},{2,6},{4,0},{6,2},{1,5},{3,7},{5,1},{7,3},{8,12},{10,14},{12... | collective-permute-start | bytes 946184 | tf_op jit(solution)/shard_map/ppermute | solution.py:21
  28.0 3.1 %collective-permute-start.2 = (bf16[176,896]{1,0:T(8,128)(2,1)}, bf16[176,896]{1,0:T(8,128)(2,1)S(1)}, u32[]{:S(2)}, u32[]{:S(2)}) collective-permute-start(bf16[176,896]{1,0:T(8,128)(2,1)} %bitcast.2.refs_0_), channel_id=1, source_target_pairs={{0,6},{2,0},{4,2},{6,4},{1,7},{3,1},{5,3},{7,5},{8,14},{10,8},{12,... | collective-permute-start | bytes 946184 | tf_op jit(solution)/shard_map/ppermute | solution.py:21
  31.0 0.0 copy-done
  31.0 1.5 %fusion.2.refs_9_ = bf16[896,512]{1,0:T(8,128)(2,1)S(1)} fusion(bf16[1,896,512]{2,1,0:T(8,128)(2,1)} %param.8, bf16[1,896,512]{2,1,0:T(8,128)(2,1)S(1)} %copy-done), kind=kLoop, calls=%fused_computation.5 | loop fusion | flops 2293760 | bytes 2752512 | tf_op jit(solution)/shard_map/convert_element_type | solution.py:123
  32.5 10.2 %collective-permute-start.1 = (bf16[336,512]{1,0:T(8,128)(2,1)S(1)}, bf16[336,512]{1,0:T(8,128)(2,1)S(1)}, u32[]{:S(2)}, u32[]{:S(2)}) collective-permute-start(bf16[336,512]{1,0:T(8,128)(2,1)S(1)} %slice.29), channel_id=1, source_target_pairs={{0,384},{128,0},{256,128},{384,256},{1,385},{129,1},{257,129},{385... | collective-permute-start | bytes 1032200 | tf_op jit(solution)/shard_map/ppermute | solution.py:21
  42.7 0.0 collective-permute-done.5.refs_4_
  42.7 0.0 copy-start.4
  42.8 1.9 %collective-permute-start = (bf16[336,512]{1,0:T(8,128)(2,1)S(1)}, bf16[336,512]{1,0:T(8,128)(2,1)}, u32[]{:S(2)}, u32[]{:S(2)}) collective-permute-start(bf16[336,512]{1,0:T(8,128)(2,1)S(1)} %slice.29), channel_id=1, source_target_pairs={{0,128},{128,256},{256,384},{384,0},{1,129},{129,257},{257,385},{3... | collective-permute-start | bytes 1032200 | tf_op jit(solution)/shard_map/ppermute | solution.py:21
  44.7 0.0 collective-permute-done.4.refs_3_
  44.7 0.0 copy-start.6
  44.7 3.0 %collective-permute-start.8 = (bf16[176,896]{1,0:T(8,128)(2,1)S(1)}, bf16[176,896]{1,0:T(8,128)(2,1)S(1)}, u32[]{:S(2)}, u32[]{:S(2)}) collective-permute-start(bf16[176,896]{1,0:T(8,128)(2,1)S(1)} %collective-permute-done.4.refs_3_), channel_id=1, source_target_pairs={{0,1},{1,0},{2,3},{3,2},{4,5},{5,4},{6,7},{7,6},{8,9},{9,8},{10,11... | collective-permute-start | bytes 946184 | tf_op jit(solution)/shard_map/ppermute | solution.py:21
  47.8 0.0 collective-permute-done.3.refs_2_
  47.8 1.9 %collective-permute-start.7 = (bf16[176,896]{1,0:T(8,128)(2,1)S(1)}, bf16[176,896]{1,0:T(8,128)(2,1)S(1)}, u32[]{:S(2)}, u32[]{:S(2)}) collective-permute-start(bf16[176,896]{1,0:T(8,128)(2,1)S(1)} %collective-permute-done.3.refs_2_), channel_id=1, source_target_pairs={{0,1},{1,0},{2,3},{3,2},{4,5},{5,4},{6,7},{7,6},{8,9},{9,8},{10,11... | collective-permute-start | bytes 946184 | tf_op jit(solution)/shard_map/ppermute | solution.py:21
  49.7 0.0 collective-permute-done.2.refs_1_
  49.7 0.0 copy-start.10
  49.7 2.4 %collective-permute-start.6 = (bf16[176,896]{1,0:T(8,128)(2,1)S(1)}, bf16[176,896]{1,0:T(8,128)(2,1)S(1)}, u32[]{:S(2)}, u32[]{:S(2)}) collective-permute-start(bf16[176,896]{1,0:T(8,128)(2,1)S(1)} %collective-permute-done.2.refs_1_), channel_id=1, source_target_pairs={{0,1},{1,0},{2,3},{3,2},{4,5},{5,4},{6,7},{7,6},{8,9},{9,8},{10,11... | collective-permute-start | bytes 946184 | tf_op jit(solution)/shard_map/ppermute | solution.py:21
  52.1 0.0 collective-permute-done.8.refs_7_
  52.2 0.0 collective-permute-done.7.refs_6_
  52.2 1.2 collective-permute-done.6.refs_5_
  53.4 3.9 %forward.1 = bf16[16,88,512]{2,1,0:T(8,128)(2,1)} custom-call(bf16[176,896]{1,0:T(8,128)(2,1)} %bitcast.2.refs_0_, bf16[176,896]{1,0:T(8,128)(2,1)S(1)} %collective-permute-done.2.refs_1_, bf16[176,896]{1,0:T(8,128)(2,1)S(1)} %collective-permute-done.3.refs_2_, bf16[176,896]{1,0:T(8,128)(2,1)S(1)} %collective-permute-done.4.refs_3_, ...), custom_call_target="tpu_custom_call" | custom-call | tf_op jit(solution)/shard_map/forward/pallas_call | solution.py:63
  57.3 0.0 copy-done.10
  57.3 0.0 copy-done.12
  57.3 0.0 copy-done.14
  57.3 0.0 copy-done.16
  57.3 0.0 collective-permute-done.1
  57.3 0.7 copy-done.20
  58.1 0.0 collective-permute-done
  58.1 0.0 all-to-all-done.1.u
  58.1 13.1 %all-to-all-start = ((bf16[16,88,512]{2,1,0:T(8,128)(2,1)}), bf16[16,88,512]{2,1,0:T(8,128)(2,1)}, u32[]{:S(2)}, u32[]{:S(2)}) async-start(bf16[16,88,512]{2,1,0:T(8,128)(2,1)} %forward.1), calls=%async_computation | async-start | bytes 2883584 | tf_op jit(solution)/shard_map/all_to_all | solution.py:25
  71.1 2.3 %backward.1 = (bf16[4,176,896]{2,1,0:T(8,128)(2,1)S(1)}, bf16[4,176,896]{2,1,0:T(8,128)(2,1)S(1)}, bf16[8,176,512]{2,1,0:T(8,128)(2,1)S(1)}) custom-call(bf16[8,2,88,512]{3,2,1,0:T(8,128)(2,1)S(1)} %all-to-all-done.1.u, bf16[896,512]{1,0:T(8,128)(2,1)S(1)} %bitcast.30), custom_call_target="tpu_custom_call" | custom-call | tf_op jit(solution)/shard_map/backward/pallas_call | solution.py:86
  73.5 2.9 %collective-permute-start.10 = (bf16[4,176,896]{2,1,0:T(8,128)(2,1)S(1)}, bf16[4,176,896]{2,1,0:T(8,128)(2,1)S(1)}, u32[]{:S(2)}, u32[]{:S(2)}) collective-permute-start(bf16[4,176,896]{2,1,0:T(8,128)(2,1)S(1)} %get-tuple-element.15), channel_id=1, source_target_pairs={{0,1},{1,0},{2,3},{3,2},{4,5},{5,4},{6,7},{7,6},{8,9},{9,8},{10,11... | collective-permute-start | bytes 3784712 | tf_op jit(solution)/shard_map/ppermute | solution.py:21
  76.4 0.8 slice.31
  77.2 2.0 %collective-permute-start.12 = (bf16[560,512]{1,0:T(8,128)(2,1)}, bf16[560,512]{1,0:T(8,128)(2,1)}, u32[]{:S(2)}, u32[]{:S(2)}) collective-permute-start(bf16[560,512]{1,0:T(8,128)(2,1)} %slice.31), channel_id=1, source_target_pairs={{0,384},{128,0},{256,128},{384,256},{1,385},{129,1},{257,129},{385... | collective-permute-start | bytes 1720328 | tf_op jit(solution)/shard_map/ppermute | solution.py:21
  79.2 4.2 %collective-permute-start.11 = (bf16[560,512]{1,0:T(8,128)(2,1)}, bf16[560,512]{1,0:T(8,128)(2,1)}, u32[]{:S(2)}, u32[]{:S(2)}) collective-permute-start(bf16[560,512]{1,0:T(8,128)(2,1)} %slice.31), channel_id=1, source_target_pairs={{0,128},{128,256},{256,384},{384,0},{1,129},{129,257},{257,385},{3... | collective-permute-start | bytes 1720328 | tf_op jit(solution)/shard_map/ppermute | solution.py:21
  83.4 0.0 collective-permute-done.10
  83.4 0.0 copy-start.21
  83.4 1.8 %convert_add_fusion = (f32[4,176,896]{2,1,0:T(8,128)}, bf16[4,176,896]{2,1,0:T(8,128)(2,1)S(1)}) fusion(bf16[4,176,896]{2,1,0:T(8,128)(2,1)S(1)} %get-tuple-element.16, bf16[4,176,896]{2,1,0:T(8,128)(2,1)S(1)} %collective-permute-done.10), kind=kLoop, calls=%fused_computation | loop fusion | flops 2523136 | bytes 6307840 | tf_op jit(solution)/shard_map/add | solution.py:139
  85.2 0.0 copy-start.18
  85.3 1.0 slice_bitcast_fusion.1
  86.2 2.0 %collective-permute-start.15 = (bf16[176,896]{1,0:T(8,128)(2,1)}, bf16[176,896]{1,0:T(8,128)(2,1)}, u32[]{:S(2)}, u32[]{:S(2)}) collective-permute-start(bf16[176,896]{1,0:T(8,128)(2,1)} %get-tuple-element.27), channel_id=1, source_target_pairs={{0,6},{2,0},{4,2},{6,4},{1,7},{3,1},{5,3},{7,5},{8,14},{10,8},{12,... | collective-permute-start | bytes 946184 | tf_op jit(solution)/shard_map/ppermute | solution.py:21
  88.3 4.0 %collective-permute-start.14 = (bf16[176,896]{1,0:T(8,128)(2,1)}, bf16[176,896]{1,0:T(8,128)(2,1)}, u32[]{:S(2)}, u32[]{:S(2)}) collective-permute-start(bf16[176,896]{1,0:T(8,128)(2,1)} %get-tuple-element.28), channel_id=1, source_target_pairs={{0,4},{2,6},{4,0},{6,2},{1,5},{3,7},{5,1},{7,3},{8,12},{10,14},{12... | collective-permute-start | bytes 946184 | tf_op jit(solution)/shard_map/ppermute | solution.py:21
  92.3 1.9 %collective-permute-start.13 = (bf16[176,896]{1,0:T(8,128)(2,1)}, bf16[176,896]{1,0:T(8,128)(2,1)}, u32[]{:S(2)}, u32[]{:S(2)}) collective-permute-start(bf16[176,896]{1,0:T(8,128)(2,1)} %get-tuple-element.29), channel_id=1, source_target_pairs={{0,2},{2,4},{4,6},{6,0},{1,3},{3,5},{5,7},{7,1},{8,10},{10,12},{12... | collective-permute-start | bytes 946184 | tf_op jit(solution)/shard_map/ppermute | solution.py:21
  94.2 1.1 convert_add_fusion.2
  95.4 4.9 %step.1 = f32[896,512]{1,0:T(8,128)S(1)} custom-call(bf16[176,896]{1,0:T(8,128)(2,1)} %bitcast.2.refs_0_, bf16[176,896]{1,0:T(8,128)(2,1)S(1)} %copy-done.11, bf16[176,896]{1,0:T(8,128)(2,1)S(1)} %copy-done.9, bf16[176,896]{1,0:T(8,128)(2,1)S(1)} %copy-done.7, bf16[176,896]{1,0:T(8,128)(2,1)S(1)} %copy-done.5, bf16[176,896]{1,0:T(8,128)(2,1)S(1)} %copy-done.17, ...), custom_call_target="tpu_custom_call" | custom-call | tf_op jit(solution)/shard_map/step/pallas_call | solution.py:107
  100.3 1.3 %copy-done.1 = f32[896,512]{1,0:T(8,128)} copy-done((f32[896,512]{1,0:T(8,128)}, f32[896,512]{1,0:T(8,128)S(1)}, u32[]{:S(2)}) %copy-start.1) | copy-done | bytes 1835032
  101.6 2.6 %all-to-all-done = bf16[16,88,512]{2,1,0:T(8,128)(2,1)} async-done(((bf16[16,88,512]{2,1,0:T(8,128)(2,1)}), bf16[16,88,512]{2,1,0:T(8,128)(2,1)}, u32[]{:S(2)}, u32[]{:S(2)}) %all-to-all-start) | async-done | bytes 1441824 | tf_op jit(solution)/shard_map/all_to_all | solution.py:25
  104.2 2.4 %reduce_sum.12 = bf16[88,512]{1,0:T(8,128)(2,1)} reduce(bf16[16,88,512]{2,1,0:T(8,128)(2,1)} %all-to-all-done, bf16[]{:T(256)} %constant.6.clone.1), dimensions={0}, to_apply=%region_0.0 | reduce | flops 675840 | bytes 1531906 | tf_op jit(solution)/shard_map/reduce_sum | solution.py:136
  106.5 0.0 collective-permute-done.12
  106.5 12.4 %collective-permute-done.11 = bf16[560,512]{1,0:T(8,128)(2,1)} collective-permute-done((bf16[560,512]{1,0:T(8,128)(2,1)}, bf16[560,512]{1,0:T(8,128)(2,1)}, u32[]{:S(2)}, u32[]{:S(2)}) %collective-permute-start.11) | collective-permute-done | bytes 573472 | tf_op jit(solution)/shard_map/ppermute | solution.py:21
  118.9 0.0 collective-permute-done.15
  118.9 0.0 collective-permute-done.14
  118.9 0.0 collective-permute-done.13
  118.9 1.4 %convert_add_fusion.1 = f32[560,512]{1,0:T(8,128)S(1)} fusion(bf16[560,512]{1,0:T(8,128)(2,1)} %collective-permute-done.12, bf16[560,512]{1,0:T(8,128)(2,1)} %collective-permute-done.11), kind=kLoop, calls=%fused_computation.6 | loop fusion | flops 860160 | bytes 2293760 | tf_op jit(solution)/shard_map/add | solution.py:145
  120.3 1.4 %fusion.3 = bf16[1,896,512]{2,1,0:T(8,128)(2,1)} fusion(f32[896,512]{1,0:T(8,128)S(1)} %copy-done.2, f32[560,512]{1,0:T(8,128)S(1)} %convert_add_fusion.1, f32[336,512]{1,0:T(8,128)S(1)} %convert_add_fusion.2), kind=kLoop, calls=%fused_computation.7 | loop fusion | flops 1835008 | bytes 4587520 | tf_op jit(solution)/shard_map/broadcast_in_dim | solution.py:147
  121.7 2.2 %fusion.6 = bf16[1,176,896]{2,1,0:T(8,128)(2,1)} fusion(bf16[176,896]{1,0:T(8,128)(2,1)} %collective-permute-done.15, bf16[176,896]{1,0:T(8,128)(2,1)} %collective-permute-done.14, bf16[176,896]{1,0:T(8,128)(2,1)} %collective-permute-done.13, f32[4,176,896]{2,1,0:T(8,128)} %get-tuple-element.25), kind=kLoop, calls=%fused_computation.12 | loop fusion | flops 1103872 | bytes 1892352 | tf_op jit(solution)/shard_map/broadcast_in_dim | solution.py:147
  (30 shorter events, 0.1 us)
Async XLA Ops:
  0.6 7.0 %collective-permute-start.9 = (bf16[88,512]{1,0:T(8,128)(2,1)}, bf16[88,512]{1,0:T(8,128)(2,1)S(1)}, u32[]{:S(2)}, u32[]{:S(2)}) collective-permute-start(bf16[88,512]{1,0:T(8,128)(2,1)} %bitcast.33), channel_id=1, source_target_pairs={{0,64},{64,0},{1,65},{65,1},{2,66},{66,2},{3,67},{67,3},{4,68},{68... | collective-permute-start | bytes 270344 | tf_op jit(solution)/shard_map/ppermute | solution.py:21
  7.6 0.9 copy-start.19
  8.6 1.1 copy-start.3
  9.7 21.4 %copy-start = (bf16[1,896,512]{2,1,0:T(8,128)(2,1)S(1)}, bf16[1,896,512]{2,1,0:T(8,128)(2,1)}, u32[]{:S(2)}) copy-start(bf16[1,896,512]{2,1,0:T(8,128)(2,1)} %param.7) | copy-start | bytes 2752516
  9.7 48.4 %all-to-all-start.1 = ((bf16[8,2,88,512]{3,2,1,0:T(8,128)(2,1)}), bf16[8,2,88,512]{3,2,1,0:T(8,128)(2,1)S(1)}, u32[]{:S(2)}, u32[]{:S(2)}) async-start(bf16[8,2,88,512]{3,2,1,0:T(8,128)(2,1)} %copy-done.3), calls=%async_computation.1 | async-start | bytes 2883584 | tf_op jit(solution)/shard_map/all_to_all | solution.py:25
  17.1 25.7 %collective-permute-start.5 = (bf16[176,896]{1,0:T(8,128)(2,1)}, bf16[176,896]{1,0:T(8,128)(2,1)S(1)}, u32[]{:S(2)}, u32[]{:S(2)}) collective-permute-start(bf16[176,896]{1,0:T(8,128)(2,1)} %bitcast.2.refs_0_), channel_id=1, source_target_pairs={{0,1},{1,0},{2,3},{3,2},{4,5},{5,4},{6,7},{7,6},{8,9},{9,8},{10,11... | collective-permute-start | bytes 946184 | tf_op jit(solution)/shard_map/ppermute | solution.py:21
  21.9 22.8 %collective-permute-start.4 = (bf16[176,896]{1,0:T(8,128)(2,1)}, bf16[176,896]{1,0:T(8,128)(2,1)S(1)}, u32[]{:S(2)}, u32[]{:S(2)}) collective-permute-start(bf16[176,896]{1,0:T(8,128)(2,1)} %bitcast.2.refs_0_), channel_id=1, source_target_pairs={{0,2},{2,4},{4,6},{6,0},{1,3},{3,5},{5,7},{7,1},{8,10},{10,12},{12... | collective-permute-start | bytes 946184 | tf_op jit(solution)/shard_map/ppermute | solution.py:21
  23.8 24.0 %collective-permute-start.3 = (bf16[176,896]{1,0:T(8,128)(2,1)}, bf16[176,896]{1,0:T(8,128)(2,1)S(1)}, u32[]{:S(2)}, u32[]{:S(2)}) collective-permute-start(bf16[176,896]{1,0:T(8,128)(2,1)} %bitcast.2.refs_0_), channel_id=1, source_target_pairs={{0,4},{2,6},{4,0},{6,2},{1,5},{3,7},{5,1},{7,3},{8,12},{10,14},{12... | collective-permute-start | bytes 946184 | tf_op jit(solution)/shard_map/ppermute | solution.py:21
  28.0 21.7 %collective-permute-start.2 = (bf16[176,896]{1,0:T(8,128)(2,1)}, bf16[176,896]{1,0:T(8,128)(2,1)S(1)}, u32[]{:S(2)}, u32[]{:S(2)}) collective-permute-start(bf16[176,896]{1,0:T(8,128)(2,1)} %bitcast.2.refs_0_), channel_id=1, source_target_pairs={{0,6},{2,0},{4,2},{6,4},{1,7},{3,1},{5,3},{7,5},{8,14},{10,8},{12,... | collective-permute-start | bytes 946184 | tf_op jit(solution)/shard_map/ppermute | solution.py:21
  32.5 24.8 %collective-permute-start.1 = (bf16[336,512]{1,0:T(8,128)(2,1)S(1)}, bf16[336,512]{1,0:T(8,128)(2,1)S(1)}, u32[]{:S(2)}, u32[]{:S(2)}) collective-permute-start(bf16[336,512]{1,0:T(8,128)(2,1)S(1)} %slice.29), channel_id=1, source_target_pairs={{0,384},{128,0},{256,128},{384,256},{1,385},{129,1},{257,129},{385... | collective-permute-start | bytes 1032200 | tf_op jit(solution)/shard_map/ppermute | solution.py:21
  42.7 14.5 %copy-start.4 = (bf16[176,896]{1,0:T(8,128)(2,1)}, bf16[176,896]{1,0:T(8,128)(2,1)S(1)}, u32[]{:S(2)}) copy-start(bf16[176,896]{1,0:T(8,128)(2,1)S(1)} %collective-permute-done.5.refs_4_) | copy-start | bytes 946180
  42.8 15.3 %collective-permute-start = (bf16[336,512]{1,0:T(8,128)(2,1)S(1)}, bf16[336,512]{1,0:T(8,128)(2,1)}, u32[]{:S(2)}, u32[]{:S(2)}) collective-permute-start(bf16[336,512]{1,0:T(8,128)(2,1)S(1)} %slice.29), channel_id=1, source_target_pairs={{0,128},{128,256},{256,384},{384,0},{1,129},{129,257},{257,385},{3... | collective-permute-start | bytes 1032200 | tf_op jit(solution)/shard_map/ppermute | solution.py:21
  44.7 12.6 %copy-start.6 = (bf16[176,896]{1,0:T(8,128)(2,1)}, bf16[176,896]{1,0:T(8,128)(2,1)S(1)}, u32[]{:S(2)}) copy-start(bf16[176,896]{1,0:T(8,128)(2,1)S(1)} %collective-permute-done.4.refs_3_) | copy-start | bytes 946180
  44.7 7.4 %collective-permute-start.8 = (bf16[176,896]{1,0:T(8,128)(2,1)S(1)}, bf16[176,896]{1,0:T(8,128)(2,1)S(1)}, u32[]{:S(2)}, u32[]{:S(2)}) collective-permute-start(bf16[176,896]{1,0:T(8,128)(2,1)S(1)} %collective-permute-done.4.refs_3_), channel_id=1, source_target_pairs={{0,1},{1,0},{2,3},{3,2},{4,5},{5,4},{6,7},{7,6},{8,9},{9,8},{10,11... | collective-permute-start | bytes 946184 | tf_op jit(solution)/shard_map/ppermute | solution.py:21
  47.8 9.5 %copy-start.8 = (bf16[176,896]{1,0:T(8,128)(2,1)}, bf16[176,896]{1,0:T(8,128)(2,1)S(1)}, u32[]{:S(2)}) copy-start(bf16[176,896]{1,0:T(8,128)(2,1)S(1)} %collective-permute-done.3.refs_2_) | copy-start | bytes 946180
  47.8 4.4 %collective-permute-start.7 = (bf16[176,896]{1,0:T(8,128)(2,1)S(1)}, bf16[176,896]{1,0:T(8,128)(2,1)S(1)}, u32[]{:S(2)}, u32[]{:S(2)}) collective-permute-start(bf16[176,896]{1,0:T(8,128)(2,1)S(1)} %collective-permute-done.3.refs_2_), channel_id=1, source_target_pairs={{0,1},{1,0},{2,3},{3,2},{4,5},{5,4},{6,7},{7,6},{8,9},{9,8},{10,11... | collective-permute-start | bytes 946184 | tf_op jit(solution)/shard_map/ppermute | solution.py:21
  49.7 7.6 %copy-start.10 = (bf16[176,896]{1,0:T(8,128)(2,1)}, bf16[176,896]{1,0:T(8,128)(2,1)S(1)}, u32[]{:S(2)}) copy-start(bf16[176,896]{1,0:T(8,128)(2,1)S(1)} %collective-permute-done.2.refs_1_) | copy-start | bytes 946180
  49.7 3.6 %collective-permute-start.6 = (bf16[176,896]{1,0:T(8,128)(2,1)S(1)}, bf16[176,896]{1,0:T(8,128)(2,1)S(1)}, u32[]{:S(2)}, u32[]{:S(2)}) collective-permute-start(bf16[176,896]{1,0:T(8,128)(2,1)S(1)} %collective-permute-done.2.refs_1_), channel_id=1, source_target_pairs={{0,1},{1,0},{2,3},{3,2},{4,5},{5,4},{6,7},{7,6},{8,9},{9,8},{10,11... | collective-permute-start | bytes 946184 | tf_op jit(solution)/shard_map/ppermute | solution.py:21
  52.1 5.1 %copy-start.12 = (bf16[176,896]{1,0:T(8,128)(2,1)}, bf16[176,896]{1,0:T(8,128)(2,1)S(1)}, u32[]{:S(2)}) copy-start(bf16[176,896]{1,0:T(8,128)(2,1)S(1)} %collective-permute-done.8.refs_7_) | copy-start | bytes 946180
  52.2 5.1 %copy-start.14 = (bf16[176,896]{1,0:T(8,128)(2,1)}, bf16[176,896]{1,0:T(8,128)(2,1)S(1)}, u32[]{:S(2)}) copy-start(bf16[176,896]{1,0:T(8,128)(2,1)S(1)} %collective-permute-done.7.refs_6_) | copy-start | bytes 946180
  53.4 3.9 %copy-start.16 = (bf16[176,896]{1,0:T(8,128)(2,1)}, bf16[176,896]{1,0:T(8,128)(2,1)S(1)}, u32[]{:S(2)}) copy-start(bf16[176,896]{1,0:T(8,128)(2,1)S(1)} %collective-permute-done.6.refs_5_) | copy-start | bytes 946180
  57.3 0.7 copy-start.20
  58.1 46.1 %all-to-all-start = ((bf16[16,88,512]{2,1,0:T(8,128)(2,1)}), bf16[16,88,512]{2,1,0:T(8,128)(2,1)}, u32[]{:S(2)}, u32[]{:S(2)}) async-start(bf16[16,88,512]{2,1,0:T(8,128)(2,1)} %forward.1), calls=%async_computation | async-start | bytes 2883584 | tf_op jit(solution)/shard_map/all_to_all | solution.py:25
  73.5 9.9 %collective-permute-start.10 = (bf16[4,176,896]{2,1,0:T(8,128)(2,1)S(1)}, bf16[4,176,896]{2,1,0:T(8,128)(2,1)S(1)}, u32[]{:S(2)}, u32[]{:S(2)}) collective-permute-start(bf16[4,176,896]{2,1,0:T(8,128)(2,1)S(1)} %get-tuple-element.15), channel_id=1, source_target_pairs={{0,1},{1,0},{2,3},{3,2},{4,5},{5,4},{6,7},{7,6},{8,9},{9,8},{10,11... | collective-permute-start | bytes 3784712 | tf_op jit(solution)/shard_map/ppermute | solution.py:21
  77.2 29.3 %collective-permute-start.12 = (bf16[560,512]{1,0:T(8,128)(2,1)}, bf16[560,512]{1,0:T(8,128)(2,1)}, u32[]{:S(2)}, u32[]{:S(2)}) collective-permute-start(bf16[560,512]{1,0:T(8,128)(2,1)} %slice.31), channel_id=1, source_target_pairs={{0,384},{128,0},{256,128},{384,256},{1,385},{129,1},{257,129},{385... | collective-permute-start | bytes 1720328 | tf_op jit(solution)/shard_map/ppermute | solution.py:21
  79.2 39.7 %collective-permute-start.11 = (bf16[560,512]{1,0:T(8,128)(2,1)}, bf16[560,512]{1,0:T(8,128)(2,1)}, u32[]{:S(2)}, u32[]{:S(2)}) collective-permute-start(bf16[560,512]{1,0:T(8,128)(2,1)} %slice.31), channel_id=1, source_target_pairs={{0,128},{128,256},{256,384},{384,0},{1,129},{129,257},{257,385},{3... | collective-permute-start | bytes 1720328 | tf_op jit(solution)/shard_map/ppermute | solution.py:21
  83.4 10.8 %copy-start.21 = (bf16[336,512]{1,0:T(8,128)(2,1)S(1)}, bf16[336,512]{1,0:T(8,128)(2,1)}, u32[]{:S(2)}) copy-start(bf16[336,512]{1,0:T(8,128)(2,1)} %copy-done.20) | copy-start | bytes 1032196
  85.2 10.1 %copy-start.5 = (bf16[176,896]{1,0:T(8,128)(2,1)S(1)}, bf16[176,896]{1,0:T(8,128)(2,1)}, u32[]{:S(2)}) copy-start(bf16[176,896]{1,0:T(8,128)(2,1)} %copy-done.4) | copy-start | bytes 946180
  85.2 10.1 %copy-start.7 = (bf16[176,896]{1,0:T(8,128)(2,1)S(1)}, bf16[176,896]{1,0:T(8,128)(2,1)}, u32[]{:S(2)}) copy-start(bf16[176,896]{1,0:T(8,128)(2,1)} %copy-done.6) | copy-start | bytes 946180
  85.2 10.1 %copy-start.9 = (bf16[176,896]{1,0:T(8,128)(2,1)S(1)}, bf16[176,896]{1,0:T(8,128)(2,1)}, u32[]{:S(2)}) copy-start(bf16[176,896]{1,0:T(8,128)(2,1)} %copy-done.8) | copy-start | bytes 946180
  85.2 10.1 %copy-start.11 = (bf16[176,896]{1,0:T(8,128)(2,1)S(1)}, bf16[176,896]{1,0:T(8,128)(2,1)}, u32[]{:S(2)}) copy-start(bf16[176,896]{1,0:T(8,128)(2,1)} %copy-done.10) | copy-start | bytes 946180
  85.2 10.1 %copy-start.13 = (bf16[176,896]{1,0:T(8,128)(2,1)S(1)}, bf16[176,896]{1,0:T(8,128)(2,1)}, u32[]{:S(2)}) copy-start(bf16[176,896]{1,0:T(8,128)(2,1)} %copy-done.12) | copy-start | bytes 946180
  85.2 10.1 %copy-start.15 = (bf16[176,896]{1,0:T(8,128)(2,1)S(1)}, bf16[176,896]{1,0:T(8,128)(2,1)}, u32[]{:S(2)}) copy-start(bf16[176,896]{1,0:T(8,128)(2,1)} %copy-done.14) | copy-start | bytes 946180
  85.2 10.1 %copy-start.17 = (bf16[176,896]{1,0:T(8,128)(2,1)S(1)}, bf16[176,896]{1,0:T(8,128)(2,1)}, u32[]{:S(2)}) copy-start(bf16[176,896]{1,0:T(8,128)(2,1)} %copy-done.16) | copy-start | bytes 946180
  85.2 10.1 %copy-start.18 = (bf16[1,896,512]{2,1,0:T(8,128)(2,1)S(1)}, bf16[1,896,512]{2,1,0:T(8,128)(2,1)}, u32[]{:S(2)}) copy-start(bf16[1,896,512]{2,1,0:T(8,128)(2,1)} %param.9) | copy-start | bytes 2752516
  86.2 32.7 %collective-permute-start.15 = (bf16[176,896]{1,0:T(8,128)(2,1)}, bf16[176,896]{1,0:T(8,128)(2,1)}, u32[]{:S(2)}, u32[]{:S(2)}) collective-permute-start(bf16[176,896]{1,0:T(8,128)(2,1)} %get-tuple-element.27), channel_id=1, source_target_pairs={{0,6},{2,0},{4,2},{6,4},{1,7},{3,1},{5,3},{7,5},{8,14},{10,8},{12,... | collective-permute-start | bytes 946184 | tf_op jit(solution)/shard_map/ppermute | solution.py:21
  88.3 30.6 %collective-permute-start.14 = (bf16[176,896]{1,0:T(8,128)(2,1)}, bf16[176,896]{1,0:T(8,128)(2,1)}, u32[]{:S(2)}, u32[]{:S(2)}) collective-permute-start(bf16[176,896]{1,0:T(8,128)(2,1)} %get-tuple-element.28), channel_id=1, source_target_pairs={{0,4},{2,6},{4,0},{6,2},{1,5},{3,7},{5,1},{7,3},{8,12},{10,14},{12... | collective-permute-start | bytes 946184 | tf_op jit(solution)/shard_map/ppermute | solution.py:21
  92.3 26.6 %collective-permute-start.13 = (bf16[176,896]{1,0:T(8,128)(2,1)}, bf16[176,896]{1,0:T(8,128)(2,1)}, u32[]{:S(2)}, u32[]{:S(2)}) collective-permute-start(bf16[176,896]{1,0:T(8,128)(2,1)} %get-tuple-element.29), channel_id=1, source_target_pairs={{0,2},{2,4},{4,6},{6,0},{1,3},{3,5},{5,7},{7,1},{8,10},{10,12},{12... | collective-permute-start | bytes 946184 | tf_op jit(solution)/shard_map/ppermute | solution.py:21
  100.3 1.3 %copy-start.1 = (f32[896,512]{1,0:T(8,128)}, f32[896,512]{1,0:T(8,128)S(1)}, u32[]{:S(2)}) copy-start(f32[896,512]{1,0:T(8,128)S(1)} %step.1) | copy-start | bytes 5505028
  104.2 16.1 %copy-start.2 = (f32[896,512]{1,0:T(8,128)S(1)}, f32[896,512]{1,0:T(8,128)}, u32[]{:S(2)}) copy-start(f32[896,512]{1,0:T(8,128)} %copy-done.1) | copy-start | bytes 5505028

commit v2 on v1

v2 whole, which is shorter than its diff:
```python
import jax
import jax.numpy as jnp
from jax import lax
from jax.experimental import pallas as pl
from jax.experimental.pallas import tpu as pltpu
from jax.sharding import Mesh
from jax.sharding import PartitionSpec as P

FF = 14336
SCALE = FF ** (-0.5)
ROW = ("z", "y")
COL = ("x", "c")
F32 = jnp.float32
BF16 = jnp.bfloat16
PARAMS = pltpu.CompilerParams(vmem_limit_bytes=16 * 2**20)
N_X = 4


def shifted(array, axis, by):
    peers = lax.axis_size(axis)
    return lax.ppermute(array, axis, [(i, (i + by) % peers) for i in range(peers)])


def exchanged(parts, axis):
    return lax.all_to_all(parts, axis, 0, 0, tiled=False)


def dot(a, b, ca, cb):
    return lax.dot_general(a, b, (((ca,), (cb,)), ((), ())), preferred_element_type=F32)


def column(d, other):
    x, c = lax.axis_index("x"), lax.axis_index("c")
    return (x + d) % N_X * 2 + (1 - c if other else c)


def pack_kernel(*refs):
    for k, ref in enumerate(refs[:-1]):
        refs[-1][k] = ref[...]


def pack(*arrays):
    return pl.pallas_call(
        pack_kernel,
        out_shape=jax.ShapeDtypeStruct((len(arrays), *arrays[0].shape), BF16),
        compiler_params=PARAMS,
        name="pack",
    )(*arrays)


def fan_kernel(u, u_z, out):
    for y in range(out.shape[0]):
        out[y, 0] = u[...]
        out[y, 1] = u_z[...]


def fan(u, u_z):
    return pl.pallas_call(
        fan_kernel,
        out_shape=pltpu.HBM((2 * N_X, 2, *u.shape), BF16),
        compiler_params=PARAMS,
        name="fan",
    )(u, u_z)


def whole(refs):
    own, far, oth, oth_far = refs
    return [own[...], *(far[k] for k in range(N_X - 1))] + [
        oth[...],
        *(oth_far[k] for k in range(N_X - 1)),
    ]


def forward_kernel(*refs):
    h, (w, out) = refs[:-2], refs[-2:]
    rows = out.shape[1]
    for k, block in enumerate(whole(h)):
        at = column(k % N_X, k >= N_X)
        term = dot(block, w[...], 1, 0) * SCALE
        out[2 * at] = term[:rows].astype(BF16)
        out[2 * at + 1] = term[rows:].astype(BF16)


def forward(h, w, rows):
    return pl.pallas_call(
        forward_kernel,
        out_shape=pltpu.HBM((4 * N_X, rows, w.shape[1]), BF16),
        compiler_params=PARAMS,
        name="forward",
    )(*h, w)


def backward_kernel(u, w, send, keep, ordered):
    for other in (1, 0):
        for d in range(N_X):
            at = column(d, other)
            y, far = 2 * at % (2 * N_X), (at // N_X + lax.axis_index("z")) % 2
            pair = [u[y + j, far].astype(F32) for j in range(2)]
            both = jnp.concatenate(pair).astype(BF16)
            ordered[other * N_X + d] = both
            term = dot(both, w[...], 1, 1) * SCALE
            (send if other else keep)[d] = term.astype(BF16)


def backward(u, w):
    rows, feats = u.shape[2:]
    half = pltpu.HBM((N_X, 2 * rows, w.shape[0]), BF16)
    return pl.pallas_call(
        backward_kernel,
        out_shape=[half, half, pltpu.HBM((2 * N_X, 2 * rows, feats), BF16)],
        compiler_params=PARAMS,
        name="backward",
    )(u, w)


def merge_kernel(got, keep, own, *outs):
    for d, out in enumerate((own, *outs)):
        out[...] = (got[d].astype(F32) + keep[d].astype(F32)).astype(out.dtype)


def merge(got, keep):
    one = got.shape[1:]
    return pl.pallas_call(
        merge_kernel,
        out_shape=[jax.ShapeDtypeStruct(one, F32)] + [jax.ShapeDtypeStruct(one, BF16)] * (N_X - 1),
        compiler_params=PARAMS,
        name="merge",
    )(got, keep)


def step_kernel(*refs):
    h, (u, blend, prev, left, right, out) = refs[:-6], refs[-6:]
    grad = dot(jnp.concatenate(whole(h)), u[...], 0, 0) * SCALE
    centre = blend[...].astype(F32)
    around = left[...].astype(F32) + centre + right[...].astype(F32)
    fresh = centre + around * (1.0 / 3.0) - 0.5 * (grad - prev[...].astype(F32))
    out[...] = fresh.astype(BF16)


def local_step(h, u, *weights):
    units, feats = weights[0].shape
    tok = h[0].shape[0]
    one = pl.BlockSpec((tok, 128), lambda i: (0, i))
    far = pl.BlockSpec((N_X - 1, tok, 128), lambda i: (0, 0, i))
    w_spec = pl.BlockSpec((128, feats), lambda i: (i, 0))
    u_spec = pl.BlockSpec(u.shape, lambda i: (0, 0))
    return pl.pallas_call(
        step_kernel,
        grid=(units // 128,),
        out_shape=jax.ShapeDtypeStruct((units, feats), BF16),
        in_specs=[one, far, one, far, u_spec] + [w_spec] * len(weights),
        out_specs=w_spec,
        compiler_params=PARAMS,
        name="step",
    )(*h, u, *weights)


def gather(h, u, u_z, w):
    far = pack(*(shifted(h, "x", -d) for d in range(1, N_X)))
    acts = (far, shifted(h, "c", 1), shifted(far, "c", 1))
    u_all = exchanged(fan(u, u_z), "y")
    return forward((h, *acts), w, u.shape[0]), u_all, *acts


def on_device(hidden, cotangent, weight, prev_weight, prev_grad):
    tok = hidden.shape[1]
    h, u, w = hidden[0], cotangent[0], weight[0]

    u_z = shifted(u, "z", 1)
    blend = (w.astype(F32) - 0.5 * prev_weight[0].astype(F32)).astype(BF16)
    blend, u_z = lax.optimization_barrier((blend, u_z))
    left, right = shifted(blend, "replica", 1), shifted(blend, "replica", -1)

    o, u_all, *acts = lax.cond(u[0, 0] == u[0, 0], gather, gather, h, u, u_z, w)
    left, right, o, u_all = lax.optimization_barrier((left, right, o, u_all))

    o = exchanged(o, ROW)
    output = o.astype(F32).sum(axis=0).astype(BF16)

    b_send, b_keep, u_rel = backward(u_all, w)
    b_own, *b_far = merge(shifted(b_send, "c", 1), b_keep)
    got = [shifted(part, "x", d) for d, part in enumerate(b_far, 1)]
    hidden_grad = (b_own + sum(part.astype(F32) for part in got)).astype(BF16)

    u_rel = u_rel.reshape(2 * N_X * tok, u.shape[1])
    fresh = local_step((h, *acts), u_rel, blend, prev_grad[0], left, right)
    return output[None], hidden_grad[None], fresh[None]


def solution(mesh):
    torus = Mesh(
        mesh.devices.reshape(mesh.shape["replica"], 2, 8, N_X, 2),
        ("replica", "z", "y", "x", "c"),
    )
    return jax.shard_map(
        on_device,
        mesh=torus,
        in_specs=(
            P("replica", COL, ROW),
            P("replica", ROW, COL),
            P("replica", ROW, COL),
            P("replica", ROW, COL),
            P("replica", ROW, COL),
        ),
        out_specs=(P("replica", ROW, COL), P("replica", COL, ROW), P("replica", ROW, COL)),
        check_vma=False,
    )
```

time: 126 us -> 111 us (0.88)
  starting transfers between devices: 75.7 us -> 55.8 us
  waiting for transfers between devices: 18.3 us -> 26.6 us
  other arithmetic: 11.7 us -> 4.83 us
  Pallas kernels: 11.2 us -> 16.8 us
  local copies, waits for them, and re-layouts: 5.93 us -> 2.8 us
    ppermute x16 -> x12, starting transfers between devices: 55.3 us -> 44.1 us  [shifted(): lax.ppermute(array, axis, [(i, (i + by) % peers) for i in range(peers)])]
    all_to_all x2, starting transfers between devices: 20.4 us -> 11.7 us  [exchanged(): return lax.all_to_all(parts, axis, 0, 0, tiled=False)]
    ppermute x16 -> x12, waiting for transfers between devices: 15.7 us -> 23.6 us  [shifted(): lax.ppermute(array, axis, [(i, (i + by) % peers) for i in range(peers)])]
    pallas_call x3 -> x5, Pallas kernels: 6.34 us -> 11.1 us  [the longest x1 5.69 us: backward(): pl.pallas_call(backward_kernel, out_shape=[half, half, pltpu.HBM((2 * N_X...]
    add x3 -> x0, other arithmetic: 4.27 us -> none  [the longest x2 2.48 us: on_device(): a.astype(F32) + b.astype(F32)]
    unnamed x44 -> x14, local copies, waits for them, and re-layouts: 4.1 us -> 1.32 us
    broadcast_in_dim x2 -> x1, other arithmetic: 3.63 us -> 0.88 us  [on_device(): return (output[None], hidden_grad[None], fresh[None])]
  transfers between devices with their start and end apart: 18 -> 14, of which waited for: 4 -> 9; matrix products, arithmetic and copies ran while one was open for 7% -> 3% of each run, Pallas kernels for 9% -> 15%
where the time goes in v2:
time: 111 us; the launch traced here: 109 us
  starting transfers between devices  55.8 us (50%)
  waiting for transfers between devices  26.6 us (24%)
  Pallas kernels  16.8 us (15%)
  other arithmetic  4.83 us (4%)
  local copies, waits for them, and re-layouts  2.8 us (3%)
  between operations  2.09 us (2%)
    ppermute x12, starting transfers between devices, shifted(): lax.ppermute(array, axis, [(i, (i + by) % peers) for i in range(peers)])  44.1 us
    ppermute x12, waiting for transfers between devices, shifted(): lax.ppermute(array, axis, [(i, (i + by) % peers) for i in range(peers)])  23.6 us
    all_to_all x2, starting transfers between devices, exchanged(): return lax.all_to_all(parts, axis, 0, 0, tiled=False)  11.7 us
    pallas_call x1, Pallas kernels, local_step(): pl.pallas_call(step_kernel, grid=(units // 128,), out_shape=jax.ShapeDtyp...  5.73 us
    pallas_call x1, Pallas kernels, backward(): pl.pallas_call(backward_kernel, out_shape=[half, half, pltpu.HBM((2 * N_X...  5.69 us
    pallas_call x1, Pallas kernels, forward(): pl.pallas_call(forward_kernel, out_shape=pltpu.HBM((4 * N_X, rows, w.shap...  3.77 us
    all_to_all x2, waiting for transfers between devices, exchanged(): return lax.all_to_all(parts, axis, 0, 0, tiled=False)  3.07 us
    reduce_sum x1, other arithmetic, on_device(): output = o.astype(F32).sum(axis=0).astype(BF16)  2.22 us
  transfers between devices with their start and end apart: 14, of which 9 were waited for; matrix products, arithmetic and copies ran while one was open for 3% of the time, Pallas kernels for 15%

profile of v2, /device:TPU:1, one launch (start us, length us, event | category | flops | bytes accessed | tf_op | source)
XLA Modules:
  0.0 109.1 jit_solution(7879727241872565301)
XLA Ops:
  0.6 0.0 copy-start.12
  0.6 0.0 copy-start.11
  0.7 5.0 %collective-permute-start.10 = (bf16[88,512]{1,0:T(8,128)(2,1)}, bf16[88,512]{1,0:T(8,128)(2,1)S(1)}, u32[]{:S(2)}, u32[]{:S(2)}) collective-permute-start(bf16[88,512]{1,0:T(8,128)(2,1)} %bitcast.24), channel_id=1, source_target_pairs={{0,64},{64,0},{1,65},{65,1},{2,66},{66,2},{3,67},{67,3},{4,68},{68... | collective-permute-start | bytes 270344 | tf_op jit(solution)/shard_map/ppermute | solution.py:21
  5.6 1.7 %fusion.refs_5_ = bf16[896,512]{1,0:T(8,128)(2,1)S(1)} fusion(bf16[1,896,512]{2,1,0:T(8,128)(2,1)} %param.10, bf16[1,896,512]{2,1,0:T(8,128)(2,1)} %param.9), kind=kLoop, calls=%fused_computation.1 | loop fusion | flops 2293760 | bytes 2752512 | tf_op jit(solution)/shard_map/convert_element_type | solution.py:170
  7.4 0.4 collective-permute-done.10
  7.7 6.2 %collective-permute-start.11 = (bf16[896,512]{1,0:T(8,128)(2,1)S(1)}, bf16[896,512]{1,0:T(8,128)(2,1)S(1)}, u32[]{:S(2)}, u32[]{:S(2)}) collective-permute-start(bf16[896,512]{1,0:T(8,128)(2,1)S(1)} %fusion.refs_5_), channel_id=1, source_target_pairs={{0,128},{128,256},{256,384},{384,0},{1,129},{129,257},{257,385},{3... | collective-permute-start | bytes 2752520 | tf_op jit(solution)/shard_map/ppermute | solution.py:21
  14.0 5.7 %collective-permute-start.12 = (bf16[896,512]{1,0:T(8,128)(2,1)S(1)}, bf16[896,512]{1,0:T(8,128)(2,1)S(1)}, u32[]{:S(2)}, u32[]{:S(2)}) collective-permute-start(bf16[896,512]{1,0:T(8,128)(2,1)S(1)} %fusion.refs_5_), channel_id=1, source_target_pairs={{0,384},{128,0},{256,128},{384,256},{1,385},{129,1},{257,129},{385... | collective-permute-start | bytes 2752520 | tf_op jit(solution)/shard_map/ppermute | solution.py:21
  19.7 0.0 copy-done.12
  19.7 0.5 slice.5
  21.5 0.0 copy-done.11
  21.5 45.8 %conditional.1 = (bf16[16,88,512]{2,1,0:T(8,128)(2,1)}, bf16[8,2,88,512]{3,2,1,0:T(8,128)(2,1)}, bf16[3,176,896]{2,1,0:T(8,128)(2,1)}, bf16[176,896]{1,0:T(8,128)(2,1)}, bf16[3,176,896]{2,1,0:T(8,128)(2,1)}) conditional(s32[]{:T(128)} %bitcast.3, (bf16[176,896]{1,0:T(8,128)(2,1)S(1)}, bf16[896,512]{1,0:T(8,128)(2,1)}, bf16[88,512]{1,0:T(8,128)(2,1)S(1)}, ...), branch_computations={%region_0.0_spmd, %region_1.0_spmd} | conditional | bytes 24396132 | solution.py:174
  21.5 1.3 %fan.3 = bf16[8,2,88,512]{3,2,1,0:T(8,128)(2,1)} custom-call(bf16[88,512]{1,0:T(8,128)(2,1)S(1)} %get-tuple-element.22.u, bf16[88,512]{1,0:T(8,128)(2,1)S(1)} %get-tuple-element.23.u_z), custom_call_target="tpu_custom_call" | custom-call | tf_op jit(solution)/shard_map/cond/branch_1_fun/fan/pallas_call | solution.py:58
  22.8 6.8 %all-to-all-start.1 = ((bf16[8,2,88,512]{3,2,1,0:T(8,128)(2,1)}), bf16[8,2,88,512]{3,2,1,0:T(8,128)(2,1)}, u32[]{:S(2)}, u32[]{:S(2)}) async-start(bf16[8,2,88,512]{3,2,1,0:T(8,128)(2,1)} %fan.3), calls=%async_computation.1 | async-start | bytes 2883584 | tf_op jit(solution)/shard_map/cond/branch_1_fun/all_to_all | solution.py:25
  29.6 0.0 copy-start.7
  29.6 4.5 %collective-permute-start.5 = (bf16[176,896]{1,0:T(8,128)(2,1)S(1)}, bf16[176,896]{1,0:T(8,128)(2,1)S(1)}, u32[]{:S(2)}, u32[]{:S(2)}) collective-permute-start(bf16[176,896]{1,0:T(8,128)(2,1)S(1)} %get-tuple-element.20.refs_0_), channel_id=1, source_target_pairs={{0,6},{2,0},{4,2},{6,4},{1,7},{3,1},{5,3},{7,5},{8,14},{10,8},{12,... | collective-permute-start | bytes 946184 | tf_op jit(solution)/shard_map/cond/branch_1_fun/ppermute | solution.py:21
  34.1 2.4 %collective-permute-start.6 = (bf16[176,896]{1,0:T(8,128)(2,1)S(1)}, bf16[176,896]{1,0:T(8,128)(2,1)S(1)}, u32[]{:S(2)}, u32[]{:S(2)}) collective-permute-start(bf16[176,896]{1,0:T(8,128)(2,1)S(1)} %get-tuple-element.20.refs_0_), channel_id=1, source_target_pairs={{0,4},{2,6},{4,0},{6,2},{1,5},{3,7},{5,1},{7,3},{8,12},{10,14},{12... | collective-permute-start | bytes 946184 | tf_op jit(solution)/shard_map/cond/branch_1_fun/ppermute | solution.py:21
  36.6 2.5 %collective-permute-start.7 = (bf16[176,896]{1,0:T(8,128)(2,1)S(1)}, bf16[176,896]{1,0:T(8,128)(2,1)S(1)}, u32[]{:S(2)}, u32[]{:S(2)}) collective-permute-start(bf16[176,896]{1,0:T(8,128)(2,1)S(1)} %get-tuple-element.20.refs_0_), channel_id=1, source_target_pairs={{0,2},{2,4},{4,6},{6,0},{1,3},{3,5},{5,7},{7,1},{8,10},{10,12},{12... | collective-permute-start | bytes 946184 | tf_op jit(solution)/shard_map/cond/branch_1_fun/ppermute | solution.py:21
  39.1 0.0 collective-permute-done.5.refs_0_
  39.1 4.8 %collective-permute-done.6.refs_1_ = bf16[176,896]{1,0:T(8,128)(2,1)S(1)} collective-permute-done((bf16[176,896]{1,0:T(8,128)(2,1)S(1)}, bf16[176,896]{1,0:T(8,128)(2,1)S(1)}, u32[]{:S(2)}, u32[]{:S(2)}) %collective-permute-start.6) | collective-permute-done | bytes 315424 | tf_op jit(solution)/shard_map/cond/branch_1_fun/ppermute | solution.py:21
  43.9 8.9 %collective-permute-done.7.refs_2_ = bf16[176,896]{1,0:T(8,128)(2,1)S(1)} collective-permute-done((bf16[176,896]{1,0:T(8,128)(2,1)S(1)}, bf16[176,896]{1,0:T(8,128)(2,1)S(1)}, u32[]{:S(2)}, u32[]{:S(2)}) %collective-permute-start.7) | collective-permute-done | bytes 315424 | tf_op jit(solution)/shard_map/cond/branch_1_fun/ppermute | solution.py:21
  52.8 0.1 pack.3.refs_1_
  52.9 0.0 copy-start.4
  52.9 3.3 %collective-permute-start.9 = (bf16[3,176,896]{2,1,0:T(8,128)(2,1)S(1)}, bf16[3,176,896]{2,1,0:T(8,128)(2,1)S(1)}, u32[]{:S(2)}, u32[]{:S(2)}) collective-permute-start(bf16[3,176,896]{2,1,0:T(8,128)(2,1)S(1)} %pack.3.refs_1_), channel_id=1, source_target_pairs={{0,1},{1,0},{2,3},{3,2},{4,5},{5,4},{6,7},{7,6},{8,9},{9,8},{10,11... | collective-permute-start | bytes 2838536 | tf_op jit(solution)/shard_map/cond/branch_1_fun/ppermute | solution.py:21
  56.2 1.9 %collective-permute-start.8 = (bf16[176,896]{1,0:T(8,128)(2,1)S(1)}, bf16[176,896]{1,0:T(8,128)(2,1)}, u32[]{:S(2)}, u32[]{:S(2)}) collective-permute-start(bf16[176,896]{1,0:T(8,128)(2,1)S(1)} %get-tuple-element.20.refs_0_), channel_id=1, source_target_pairs={{0,1},{1,0},{2,3},{3,2},{4,5},{5,4},{6,7},{7,6},{8,9},{9,8},{10,11... | collective-permute-start | bytes 946184 | tf_op jit(solution)/shard_map/cond/branch_1_fun/ppermute | solution.py:21
  58.1 1.7 %collective-permute-done.8.refs_2_ = bf16[176,896]{1,0:T(8,128)(2,1)} collective-permute-done((bf16[176,896]{1,0:T(8,128)(2,1)S(1)}, bf16[176,896]{1,0:T(8,128)(2,1)}, u32[]{:S(2)}, u32[]{:S(2)}) %collective-permute-start.8) | collective-permute-done | bytes 315424 | tf_op jit(solution)/shard_map/cond/branch_1_fun/ppermute | solution.py:21
  59.8 0.0 collective-permute-done.9.refs_3_
  59.8 0.0 copy-start.9
  59.8 0.0 copy-done.4
  59.8 1.0 copy-done.9
  60.8 0.0 copy-done.7
  60.8 3.8 %forward.3 = bf16[16,88,512]{2,1,0:T(8,128)(2,1)} custom-call(bf16[176,896]{1,0:T(8,128)(2,1)S(1)} %get-tuple-element.20.refs_0_, bf16[3,176,896]{2,1,0:T(8,128)(2,1)S(1)} %pack.3.refs_1_, bf16[176,896]{1,0:T(8,128)(2,1)} %collective-permute-done.8.refs_2_, bf16[3,176,896]{2,1,0:T(8,128)(2,1)S(1)} %collective-permute-done.9.refs_3_, ...), custom_call_target="tpu_custom_call" | custom-call | tf_op jit(solution)/shard_map/cond/branch_1_fun/forward/pallas_call | solution.py:85
  64.5 2.8 %all-to-all-done.1 = bf16[8,2,88,512]{3,2,1,0:T(8,128)(2,1)} async-done(((bf16[8,2,88,512]{3,2,1,0:T(8,128)(2,1)}), bf16[8,2,88,512]{3,2,1,0:T(8,128)(2,1)}, u32[]{:S(2)}, u32[]{:S(2)}) %all-to-all-start.1) | async-done | bytes 1441824 | tf_op jit(solution)/shard_map/cond/branch_1_fun/all_to_all | solution.py:25
  67.3 0.0 collective-permute-done.11.refs_7_
  67.3 0.0 collective-permute-done.12.refs_8_
  67.3 4.9 %all-to-all-start.2 = ((bf16[16,88,512]{2,1,0:T(8,128)(2,1)}), bf16[16,88,512]{2,1,0:T(8,128)(2,1)}, u32[]{:S(2)}, u32[]{:S(2)}) async-start(bf16[16,88,512]{2,1,0:T(8,128)(2,1)} %get-tuple-element.49), calls=%async_computation.2 | async-start | bytes 2883584 | tf_op jit(solution)/shard_map/all_to_all | solution.py:25
  72.3 0.0 copy-start.2
  72.3 0.0 copy-start.5
  72.3 5.7 %backward.1 = (bf16[4,176,896]{2,1,0:T(8,128)(2,1)}, bf16[4,176,896]{2,1,0:T(8,128)(2,1)}, bf16[8,176,512]{2,1,0:T(8,128)(2,1)}) custom-call(bf16[8,2,88,512]{3,2,1,0:T(8,128)(2,1)} %get-tuple-element.50.u, bf16[896,512]{1,0:T(8,128)(2,1)} %bitcast.19), custom_call_target="tpu_custom_call" | custom-call | tf_op jit(solution)/shard_map/backward/pallas_call | solution.py:108
  78.0 0.0 copy-start
  78.0 2.5 %collective-permute-start.13 = (bf16[4,176,896]{2,1,0:T(8,128)(2,1)}, bf16[4,176,896]{2,1,0:T(8,128)(2,1)S(1)}, u32[]{:S(2)}, u32[]{:S(2)}) collective-permute-start(bf16[4,176,896]{2,1,0:T(8,128)(2,1)} %get-tuple-element.51), channel_id=1, source_target_pairs={{0,1},{1,0},{2,3},{3,2},{4,5},{5,4},{6,7},{7,6},{8,9},{9,8},{10,11... | collective-permute-start | bytes 3784712 | tf_op jit(solution)/shard_map/ppermute | solution.py:21
  80.5 2.8 %collective-permute-done.13.got = bf16[4,176,896]{2,1,0:T(8,128)(2,1)S(1)} collective-permute-done((bf16[4,176,896]{2,1,0:T(8,128)(2,1)}, bf16[4,176,896]{2,1,0:T(8,128)(2,1)S(1)}, u32[]{:S(2)}, u32[]{:S(2)}) %collective-permute-start.13) | collective-permute-done | bytes 1261600 | tf_op jit(solution)/shard_map/ppermute | solution.py:21
  83.2 0.0 copy-start.1
  83.2 1.3 %copy-done.1 = bf16[4,176,896]{2,1,0:T(8,128)(2,1)S(1)} copy-done((bf16[4,176,896]{2,1,0:T(8,128)(2,1)S(1)}, bf16[4,176,896]{2,1,0:T(8,128)(2,1)}, u32[]{:S(2)}) %copy-start.1) | copy-done | bytes 1261592
  84.5 0.0 copy-start.10
  84.5 0.3 merge.1
  84.8 2.7 %collective-permute-start.14 = (bf16[176,896]{1,0:T(8,128)(2,1)S(1)}, bf16[176,896]{1,0:T(8,128)(2,1)S(1)}, u32[]{:S(2)}, u32[]{:S(2)}) collective-permute-start(bf16[176,896]{1,0:T(8,128)(2,1)S(1)} %get-tuple-element.54), channel_id=1, source_target_pairs={{0,2},{2,4},{4,6},{6,0},{1,3},{3,5},{5,7},{7,1},{8,10},{10,12},{12... | collective-permute-start | bytes 946184 | tf_op jit(solution)/shard_map/ppermute | solution.py:21
  87.5 4.4 %collective-permute-start.15 = (bf16[176,896]{1,0:T(8,128)(2,1)S(1)}, bf16[176,896]{1,0:T(8,128)(2,1)S(1)}, u32[]{:S(2)}, u32[]{:S(2)}) collective-permute-start(bf16[176,896]{1,0:T(8,128)(2,1)S(1)} %get-tuple-element.55), channel_id=1, source_target_pairs={{0,4},{2,6},{4,0},{6,2},{1,5},{3,7},{5,1},{7,3},{8,12},{10,14},{12... | collective-permute-start | bytes 946184 | tf_op jit(solution)/shard_map/ppermute | solution.py:21
  91.9 3.1 %collective-permute-start.16 = (bf16[176,896]{1,0:T(8,128)(2,1)S(1)}, bf16[176,896]{1,0:T(8,128)(2,1)S(1)}, u32[]{:S(2)}, u32[]{:S(2)}) collective-permute-start(bf16[176,896]{1,0:T(8,128)(2,1)S(1)} %get-tuple-element.56), channel_id=1, source_target_pairs={{0,6},{2,0},{4,2},{6,4},{1,7},{3,1},{5,3},{7,5},{8,14},{10,8},{12,... | collective-permute-start | bytes 946184 | tf_op jit(solution)/shard_map/ppermute | solution.py:21
  94.9 0.0 copy-done.2
  94.9 0.0 copy-done.5
  94.9 0.0 copy-done
  94.9 0.0 copy-done.10
  95.0 5.7 %step.1 = bf16[896,512]{1,0:T(8,128)(2,1)} custom-call(bf16[176,896]{1,0:T(8,128)(2,1)S(1)} %bitcast.22, bf16[3,176,896]{2,1,0:T(8,128)(2,1)S(1)} %copy-done.5, bf16[176,896]{1,0:T(8,128)(2,1)} %get-tuple-element.58.refs_2_, bf16[3,176,896]{2,1,0:T(8,128)(2,1)S(1)} %copy-done.10, bf16[1408,512]{1,0:T(8,128)(2,1)S(1)} %bitcast.15, ...), custom_call_target="tpu_custom_call" | custom-call | tf_op jit(solution)/shard_map/step/pallas_call | solution.py:147
  100.7 0.0 collective-permute-done.14
  100.7 3.3 %collective-permute-done.15 = bf16[176,896]{1,0:T(8,128)(2,1)S(1)} collective-permute-done((bf16[176,896]{1,0:T(8,128)(2,1)S(1)}, bf16[176,896]{1,0:T(8,128)(2,1)S(1)}, u32[]{:S(2)}, u32[]{:S(2)}) %collective-permute-start.15) | collective-permute-done | bytes 315424 | tf_op jit(solution)/shard_map/ppermute | solution.py:21
  104.0 1.7 %collective-permute-done.16 = bf16[176,896]{1,0:T(8,128)(2,1)S(1)} collective-permute-done((bf16[176,896]{1,0:T(8,128)(2,1)S(1)}, bf16[176,896]{1,0:T(8,128)(2,1)S(1)}, u32[]{:S(2)}, u32[]{:S(2)}) %collective-permute-start.16) | collective-permute-done | bytes 315424 | tf_op jit(solution)/shard_map/ppermute | solution.py:21
  105.7 0.9 fusion.1
  106.5 0.3 all-to-all-done.2
  106.8 2.2 %reduce_sum.12 = bf16[88,512]{1,0:T(8,128)(2,1)} reduce(bf16[16,88,512]{2,1,0:T(8,128)(2,1)} %all-to-all-done.2, bf16[]{:T(256)} %constant.4.clone.1), dimensions={0}, to_apply=%region_2.0 | reduce | flops 675840 | bytes 1531906 | tf_op jit(solution)/shard_map/reduce_sum | solution.py:178
Async XLA Ops:
  0.6 19.0 %copy-start.12 = (bf16[1,88,512]{2,1,0:T(8,128)(2,1)S(1)}, bf16[1,88,512]{2,1,0:T(8,128)(2,1)}, u32[]{:S(2)}) copy-start(bf16[1,88,512]{2,1,0:T(8,128)(2,1)} %param.8) | copy-start | bytes 270340
  0.6 20.9 %copy-start.11 = (bf16[1,176,896]{2,1,0:T(8,128)(2,1)S(1)}, bf16[1,176,896]{2,1,0:T(8,128)(2,1)}, u32[]{:S(2)}) copy-start(bf16[1,176,896]{2,1,0:T(8,128)(2,1)} %param.7) | copy-start | bytes 946180
  0.7 7.1 %collective-permute-start.10 = (bf16[88,512]{1,0:T(8,128)(2,1)}, bf16[88,512]{1,0:T(8,128)(2,1)S(1)}, u32[]{:S(2)}, u32[]{:S(2)}) collective-permute-start(bf16[88,512]{1,0:T(8,128)(2,1)} %bitcast.24), channel_id=1, source_target_pairs={{0,64},{64,0},{1,65},{65,1},{2,66},{66,2},{3,67},{67,3},{4,68},{68... | collective-permute-start | bytes 270344 | tf_op jit(solution)/shard_map/ppermute | solution.py:21
  7.7 59.6 %collective-permute-start.11 = (bf16[896,512]{1,0:T(8,128)(2,1)S(1)}, bf16[896,512]{1,0:T(8,128)(2,1)S(1)}, u32[]{:S(2)}, u32[]{:S(2)}) collective-permute-start(bf16[896,512]{1,0:T(8,128)(2,1)S(1)} %fusion.refs_5_), channel_id=1, source_target_pairs={{0,128},{128,256},{256,384},{384,0},{1,129},{129,257},{257,385},{3... | collective-permute-start | bytes 2752520 | tf_op jit(solution)/shard_map/ppermute | solution.py:21
  14.0 53.4 %collective-permute-start.12 = (bf16[896,512]{1,0:T(8,128)(2,1)S(1)}, bf16[896,512]{1,0:T(8,128)(2,1)S(1)}, u32[]{:S(2)}, u32[]{:S(2)}) collective-permute-start(bf16[896,512]{1,0:T(8,128)(2,1)S(1)} %fusion.refs_5_), channel_id=1, source_target_pairs={{0,384},{128,0},{256,128},{384,256},{1,385},{129,1},{257,129},{385... | collective-permute-start | bytes 2752520 | tf_op jit(solution)/shard_map/ppermute | solution.py:21
  22.8 44.5 %all-to-all-start.1 = ((bf16[8,2,88,512]{3,2,1,0:T(8,128)(2,1)}), bf16[8,2,88,512]{3,2,1,0:T(8,128)(2,1)}, u32[]{:S(2)}, u32[]{:S(2)}) async-start(bf16[8,2,88,512]{3,2,1,0:T(8,128)(2,1)} %fan.3), calls=%async_computation.1 | async-start | bytes 2883584 | tf_op jit(solution)/shard_map/cond/branch_1_fun/all_to_all | solution.py:25
  29.6 31.2 %copy-start.7 = (bf16[896,512]{1,0:T(8,128)(2,1)S(1)}, bf16[896,512]{1,0:T(8,128)(2,1)}, u32[]{:S(2)}) copy-start(bf16[896,512]{1,0:T(8,128)(2,1)} %get-tuple-element.21.refs_4_) | copy-start | bytes 2752516 | tf_op jit(solution)/shard_map/cond
  29.6 9.5 %collective-permute-start.5 = (bf16[176,896]{1,0:T(8,128)(2,1)S(1)}, bf16[176,896]{1,0:T(8,128)(2,1)S(1)}, u32[]{:S(2)}, u32[]{:S(2)}) collective-permute-start(bf16[176,896]{1,0:T(8,128)(2,1)S(1)} %get-tuple-element.20.refs_0_), channel_id=1, source_target_pairs={{0,6},{2,0},{4,2},{6,4},{1,7},{3,1},{5,3},{7,5},{8,14},{10,8},{12,... | collective-permute-start | bytes 946184 | tf_op jit(solution)/shard_map/cond/branch_1_fun/ppermute | solution.py:21
  34.1 9.8 %collective-permute-start.6 = (bf16[176,896]{1,0:T(8,128)(2,1)S(1)}, bf16[176,896]{1,0:T(8,128)(2,1)S(1)}, u32[]{:S(2)}, u32[]{:S(2)}) collective-permute-start(bf16[176,896]{1,0:T(8,128)(2,1)S(1)} %get-tuple-element.20.refs_0_), channel_id=1, source_target_pairs={{0,4},{2,6},{4,0},{6,2},{1,5},{3,7},{5,1},{7,3},{8,12},{10,14},{12... | collective-permute-start | bytes 946184 | tf_op jit(solution)/shard_map/cond/branch_1_fun/ppermute | solution.py:21
  36.6 16.2 %collective-permute-start.7 = (bf16[176,896]{1,0:T(8,128)(2,1)S(1)}, bf16[176,896]{1,0:T(8,128)(2,1)S(1)}, u32[]{:S(2)}, u32[]{:S(2)}) collective-permute-start(bf16[176,896]{1,0:T(8,128)(2,1)S(1)} %get-tuple-element.20.refs_0_), channel_id=1, source_target_pairs={{0,2},{2,4},{4,6},{6,0},{1,3},{3,5},{5,7},{7,1},{8,10},{10,12},{12... | collective-permute-start | bytes 946184 | tf_op jit(solution)/shard_map/cond/branch_1_fun/ppermute | solution.py:21
  52.9 6.9 %copy-start.4 = (bf16[3,176,896]{2,1,0:T(8,128)(2,1)}, bf16[3,176,896]{2,1,0:T(8,128)(2,1)S(1)}, u32[]{:S(2)}) copy-start(bf16[3,176,896]{2,1,0:T(8,128)(2,1)S(1)} %pack.3.refs_1_) | copy-start | bytes 2838532 | tf_op jit(solution)/shard_map/cond
  52.9 6.9 %collective-permute-start.9 = (bf16[3,176,896]{2,1,0:T(8,128)(2,1)S(1)}, bf16[3,176,896]{2,1,0:T(8,128)(2,1)S(1)}, u32[]{:S(2)}, u32[]{:S(2)}) collective-permute-start(bf16[3,176,896]{2,1,0:T(8,128)(2,1)S(1)} %pack.3.refs_1_), channel_id=1, source_target_pairs={{0,1},{1,0},{2,3},{3,2},{4,5},{5,4},{6,7},{7,6},{8,9},{9,8},{10,11... | collective-permute-start | bytes 2838536 | tf_op jit(solution)/shard_map/cond/branch_1_fun/ppermute | solution.py:21
  56.2 3.6 %collective-permute-start.8 = (bf16[176,896]{1,0:T(8,128)(2,1)S(1)}, bf16[176,896]{1,0:T(8,128)(2,1)}, u32[]{:S(2)}, u32[]{:S(2)}) collective-permute-start(bf16[176,896]{1,0:T(8,128)(2,1)S(1)} %get-tuple-element.20.refs_0_), channel_id=1, source_target_pairs={{0,1},{1,0},{2,3},{3,2},{4,5},{5,4},{6,7},{7,6},{8,9},{9,8},{10,11... | collective-permute-start | bytes 946184 | tf_op jit(solution)/shard_map/cond/branch_1_fun/ppermute | solution.py:21
  59.8 1.0 copy-start.9
  67.3 39.5 %all-to-all-start.2 = ((bf16[16,88,512]{2,1,0:T(8,128)(2,1)}), bf16[16,88,512]{2,1,0:T(8,128)(2,1)}, u32[]{:S(2)}, u32[]{:S(2)}) async-start(bf16[16,88,512]{2,1,0:T(8,128)(2,1)} %get-tuple-element.49), calls=%async_computation.2 | async-start | bytes 2883584 | tf_op jit(solution)/shard_map/all_to_all | solution.py:25
  72.3 22.7 %copy-start.2 = (bf16[1,896,512]{2,1,0:T(8,128)(2,1)S(1)}, bf16[1,896,512]{2,1,0:T(8,128)(2,1)}, u32[]{:S(2)}) copy-start(bf16[1,896,512]{2,1,0:T(8,128)(2,1)} %param.11) | copy-start | bytes 2752516
  72.3 22.7 %copy-start.5 = (bf16[3,176,896]{2,1,0:T(8,128)(2,1)S(1)}, bf16[3,176,896]{2,1,0:T(8,128)(2,1)}, u32[]{:S(2)}) copy-start(bf16[3,176,896]{2,1,0:T(8,128)(2,1)} %get-tuple-element.57.refs_1_) | copy-start | bytes 2838532
  78.0 17.0 %copy-start = (bf16[8,176,512]{2,1,0:T(8,128)(2,1)S(1)}, bf16[8,176,512]{2,1,0:T(8,128)(2,1)}, u32[]{:S(2)}) copy-start(bf16[8,176,512]{2,1,0:T(8,128)(2,1)} %get-tuple-element.60) | copy-start | bytes 4325380
  78.0 5.3 %collective-permute-start.13 = (bf16[4,176,896]{2,1,0:T(8,128)(2,1)}, bf16[4,176,896]{2,1,0:T(8,128)(2,1)S(1)}, u32[]{:S(2)}, u32[]{:S(2)}) collective-permute-start(bf16[4,176,896]{2,1,0:T(8,128)(2,1)} %get-tuple-element.51), channel_id=1, source_target_pairs={{0,1},{1,0},{2,3},{3,2},{4,5},{5,4},{6,7},{7,6},{8,9},{9,8},{10,11... | collective-permute-start | bytes 3784712 | tf_op jit(solution)/shard_map/ppermute | solution.py:21
  83.2 1.3 %copy-start.1 = (bf16[4,176,896]{2,1,0:T(8,128)(2,1)S(1)}, bf16[4,176,896]{2,1,0:T(8,128)(2,1)}, u32[]{:S(2)}) copy-start(bf16[4,176,896]{2,1,0:T(8,128)(2,1)} %get-tuple-element.52.keep) | copy-start | bytes 3784708
  84.5 10.4 %copy-start.10 = (bf16[3,176,896]{2,1,0:T(8,128)(2,1)S(1)}, bf16[3,176,896]{2,1,0:T(8,128)(2,1)}, u32[]{:S(2)}) copy-start(bf16[3,176,896]{2,1,0:T(8,128)(2,1)} %get-tuple-element.59.refs_3_) | copy-start | bytes 2838532
  84.8 15.9 %collective-permute-start.14 = (bf16[176,896]{1,0:T(8,128)(2,1)S(1)}, bf16[176,896]{1,0:T(8,128)(2,1)S(1)}, u32[]{:S(2)}, u32[]{:S(2)}) collective-permute-start(bf16[176,896]{1,0:T(8,128)(2,1)S(1)} %get-tuple-element.54), channel_id=1, source_target_pairs={{0,2},{2,4},{4,6},{6,0},{1,3},{3,5},{5,7},{7,1},{8,10},{10,12},{12... | collective-permute-start | bytes 946184 | tf_op jit(solution)/shard_map/ppermute | solution.py:21
  87.5 16.5 %collective-permute-start.15 = (bf16[176,896]{1,0:T(8,128)(2,1)S(1)}, bf16[176,896]{1,0:T(8,128)(2,1)S(1)}, u32[]{:S(2)}, u32[]{:S(2)}) collective-permute-start(bf16[176,896]{1,0:T(8,128)(2,1)S(1)} %get-tuple-element.55), channel_id=1, source_target_pairs={{0,4},{2,6},{4,0},{6,2},{1,5},{3,7},{5,1},{7,3},{8,12},{10,14},{12... | collective-permute-start | bytes 946184 | tf_op jit(solution)/shard_map/ppermute | solution.py:21
  91.9 13.8 %collective-permute-start.16 = (bf16[176,896]{1,0:T(8,128)(2,1)S(1)}, bf16[176,896]{1,0:T(8,128)(2,1)S(1)}, u32[]{:S(2)}, u32[]{:S(2)}) collective-permute-start(bf16[176,896]{1,0:T(8,128)(2,1)S(1)} %get-tuple-element.56), channel_id=1, source_target_pairs={{0,6},{2,0},{4,2},{6,4},{1,7},{3,1},{5,3},{7,5},{8,14},{10,8},{12,... | collective-permute-start | bytes 946184 | tf_op jit(solution)/shard_map/ppermute | solution.py:21

commit v3 on v2

--- a/solution.py
+++ b/solution.py
@@ -155,6 +155,22 @@
     )(*h, u, *weights)
 
 
+def total_kernel(parts, out):
+    whole_sum = parts[0].astype(F32)
+    for k in range(1, parts.shape[0]):
+        whole_sum += parts[k].astype(F32)
+    out[...] = whole_sum.astype(BF16)
+
+
+def total(parts):
+    return pl.pallas_call(
+        total_kernel,
+        out_shape=jax.ShapeDtypeStruct(parts.shape[1:], BF16),
+        compiler_params=PARAMS,
+        name="total",
+    )(parts)
+
+
 def gather(h, u, u_z, w):
     far = pack(*(shifted(h, "x", -d) for d in range(1, N_X)))
     acts = (far, shifted(h, "c", 1), shifted(far, "c", 1))
@@ -168,14 +184,15 @@
 
     u_z = shifted(u, "z", 1)
     blend = (w.astype(F32) - 0.5 * prev_weight[0].astype(F32)).astype(BF16)
-    blend, u_z = lax.optimization_barrier((blend, u_z))
+    pick = u[0, 0] == u[0, 0]
+    blend, u_z, pick = lax.optimization_barrier((blend, u_z, pick))
     left, right = shifted(blend, "replica", 1), shifted(blend, "replica", -1)
 
-    o, u_all, *acts = lax.cond(u[0, 0] == u[0, 0], gather, gather, h, u, u_z, w)
+    o, u_all, *acts = lax.cond(pick, gather, gather, h, u, u_z, w)
     left, right, o, u_all = lax.optimization_barrier((left, right, o, u_all))
 
     o = exchanged(o, ROW)
-    output = o.astype(F32).sum(axis=0).astype(BF16)
+    output = total(o)
 
     b_send, b_keep, u_rel = backward(u_all, w)
     b_own, *b_far = merge(shifted(b_send, "c", 1), b_keep)

time: 111 us -> 109 us (0.982)
  Pallas kernels: 16.8 us -> 19.9 us
  other arithmetic: 4.83 us -> 2.61 us
  starting transfers between devices: 55.8 us -> 54.1 us
    reduce_sum x1 -> x0, other arithmetic: 2.22 us -> none  [on_device(): output = o.astype(F32).sum(axis=0).astype(BF16)]
    ppermute x12, starting transfers between devices: 44.1 us -> 42.5 us  [shifted(): lax.ppermute(array, axis, [(i, (i + by) % peers) for i in range(peers)])]
  transfers between devices with their start and end apart: 14 -> 14, of which waited for: 9 -> 9; matrix products, arithmetic and copies ran while one was open for 3% -> 3% of each run, Pallas kernels for 15% -> 18%
where the time goes in v3:
time: 109 us; the launch traced here: 108 us
  starting transfers between devices  54.1 us (50%)
  waiting for transfers between devices  26.1 us (24%)
  Pallas kernels  19.9 us (18%)
  local copies, waits for them, and re-layouts  2.77 us (3%)
  other arithmetic  2.61 us (2%)
  between operations  2.09 us (2%)
    ppermute x12, starting transfers between devices, shifted(): lax.ppermute(array, axis, [(i, (i + by) % peers) for i in range(peers)])  42.5 us
    ppermute x12, waiting for transfers between devices, shifted(): lax.ppermute(array, axis, [(i, (i + by) % peers) for i in range(peers)])  23.7 us
    all_to_all x2, starting transfers between devices, exchanged(): return lax.all_to_all(parts, axis, 0, 0, tiled=False)  11.5 us
    pallas_call x1, Pallas kernels, local_step(): pl.pallas_call(step_kernel, grid=(units // 128,), out_shape=jax.ShapeDtyp...  6.62 us
    pallas_call x1, Pallas kernels, backward(): pl.pallas_call(backward_kernel, out_shape=[half, half, pltpu.HBM((2 * N_X...  5.63 us
    pallas_call x1, Pallas kernels, forward(): pl.pallas_call(forward_kernel, out_shape=pltpu.HBM((4 * N_X, rows, w.shap...  4.35 us
    all_to_all x2, waiting for transfers between devices, exchanged(): return lax.all_to_all(parts, axis, 0, 0, tiled=False)  2.4 us
    unnamed x14, local copies, waits for them, and re-layouts  2.24 us
  transfers between devices with their start and end apart: 14, of which 9 were waited for; matrix products, arithmetic and copies ran while one was open for 3% of the time, Pallas kernels for 18%

profile of v3, /device:TPU:1, one launch (start us, length us, event | category | flops | bytes accessed | tf_op | source)
XLA Modules:
  0.0 107.6 jit_solution(7388597485362909597)
XLA Ops:
  0.6 0.0 copy-start.10
  0.6 5.0 %collective-permute-start.10 = (bf16[88,512]{1,0:T(8,128)(2,1)}, bf16[88,512]{1,0:T(8,128)(2,1)S(1)}, u32[]{:S(2)}, u32[]{:S(2)}) collective-permute-start(bf16[88,512]{1,0:T(8,128)(2,1)} %bitcast.24), channel_id=1, source_target_pairs={{0,64},{64,0},{1,65},{65,1},{2,66},{66,2},{3,67},{67,3},{4,68},{68... | collective-permute-start | bytes 270344 | tf_op jit(solution)/shard_map/ppermute | solution.py:21
  5.6 1.7 %fusion.refs_5_ = bf16[896,512]{1,0:T(8,128)(2,1)S(1)} fusion(bf16[1,896,512]{2,1,0:T(8,128)(2,1)} %param.10, bf16[1,896,512]{2,1,0:T(8,128)(2,1)} %param.9), kind=kLoop, calls=%fused_computation.1 | loop fusion | flops 2293760 | bytes 2752512 | tf_op jit(solution)/shard_map/convert_element_type | solution.py:186
  7.3 0.0 copy-done.10
  7.4 0.5 slice.5
  9.2 0.0 collective-permute-done.10
  9.2 5.8 %collective-permute-start.11 = (bf16[896,512]{1,0:T(8,128)(2,1)S(1)}, bf16[896,512]{1,0:T(8,128)(2,1)S(1)}, u32[]{:S(2)}, u32[]{:S(2)}) collective-permute-start(bf16[896,512]{1,0:T(8,128)(2,1)S(1)} %fusion.refs_5_), channel_id=1, source_target_pairs={{0,128},{128,256},{256,384},{384,0},{1,129},{129,257},{257,385},{3... | collective-permute-start | bytes 2752520 | tf_op jit(solution)/shard_map/ppermute | solution.py:21
  15.0 5.9 %collective-permute-start.12 = (bf16[896,512]{1,0:T(8,128)(2,1)S(1)}, bf16[896,512]{1,0:T(8,128)(2,1)S(1)}, u32[]{:S(2)}, u32[]{:S(2)}) collective-permute-start(bf16[896,512]{1,0:T(8,128)(2,1)S(1)} %fusion.refs_5_), channel_id=1, source_target_pairs={{0,384},{128,0},{256,128},{384,256},{1,385},{129,1},{257,129},{385... | collective-permute-start | bytes 2752520 | tf_op jit(solution)/shard_map/ppermute | solution.py:21
  20.9 45.8 %conditional.1 = (bf16[16,88,512]{2,1,0:T(8,128)(2,1)}, bf16[8,2,88,512]{3,2,1,0:T(8,128)(2,1)}, bf16[3,176,896]{2,1,0:T(8,128)(2,1)}, bf16[176,896]{1,0:T(8,128)(2,1)}, bf16[3,176,896]{2,1,0:T(8,128)(2,1)}) conditional(s32[]{:T(128)} %convert_element_type.28, (bf16[176,896]{1,0:T(8,128)(2,1)}, bf16[896,512]{1,0:T(8,128)(2,1)}, ...), branch_computations={%region_0.0_spmd, %region_1.0_spmd} | conditional | bytes 18088264 | solution.py:191
  20.9 1.2 %fan.3 = bf16[8,2,88,512]{3,2,1,0:T(8,128)(2,1)} custom-call(bf16[88,512]{1,0:T(8,128)(2,1)S(1)} %get-tuple-element.22.u, bf16[88,512]{1,0:T(8,128)(2,1)S(1)} %get-tuple-element.23.u_z), custom_call_target="tpu_custom_call" | custom-call | tf_op jit(solution)/shard_map/cond/branch_1_fun/fan/pallas_call | solution.py:58
  22.1 6.8 %all-to-all-start.1 = ((bf16[8,2,88,512]{3,2,1,0:T(8,128)(2,1)}), bf16[8,2,88,512]{3,2,1,0:T(8,128)(2,1)}, u32[]{:S(2)}, u32[]{:S(2)}) async-start(bf16[8,2,88,512]{3,2,1,0:T(8,128)(2,1)} %fan.3), calls=%async_computation.1 | async-start | bytes 2883584 | tf_op jit(solution)/shard_map/cond/branch_1_fun/all_to_all | solution.py:25
  28.9 0.0 copy-start.9
  28.9 0.0 copy-start.6
  28.9 4.5 %collective-permute-start.5 = (bf16[176,896]{1,0:T(8,128)(2,1)}, bf16[176,896]{1,0:T(8,128)(2,1)S(1)}, u32[]{:S(2)}, u32[]{:S(2)}) collective-permute-start(bf16[176,896]{1,0:T(8,128)(2,1)} %get-tuple-element.20.refs_0_), channel_id=1, source_target_pairs={{0,6},{2,0},{4,2},{6,4},{1,7},{3,1},{5,3},{7,5},{8,14},{10,8},{12,... | collective-permute-start | bytes 946184 | tf_op jit(solution)/shard_map/cond/branch_1_fun/ppermute | solution.py:21
  33.5 2.4 %collective-permute-start.6 = (bf16[176,896]{1,0:T(8,128)(2,1)}, bf16[176,896]{1,0:T(8,128)(2,1)S(1)}, u32[]{:S(2)}, u32[]{:S(2)}) collective-permute-start(bf16[176,896]{1,0:T(8,128)(2,1)} %get-tuple-element.20.refs_0_), channel_id=1, source_target_pairs={{0,4},{2,6},{4,0},{6,2},{1,5},{3,7},{5,1},{7,3},{8,12},{10,14},{12... | collective-permute-start | bytes 946184 | tf_op jit(solution)/shard_map/cond/branch_1_fun/ppermute | solution.py:21
  35.9 2.5 %collective-permute-start.7 = (bf16[176,896]{1,0:T(8,128)(2,1)}, bf16[176,896]{1,0:T(8,128)(2,1)S(1)}, u32[]{:S(2)}, u32[]{:S(2)}) collective-permute-start(bf16[176,896]{1,0:T(8,128)(2,1)} %get-tuple-element.20.refs_0_), channel_id=1, source_target_pairs={{0,2},{2,4},{4,6},{6,0},{1,3},{3,5},{5,7},{7,1},{8,10},{10,12},{12... | collective-permute-start | bytes 946184 | tf_op jit(solution)/shard_map/cond/branch_1_fun/ppermute | solution.py:21
  38.4 1.3 %collective-permute-done.5.refs_0_ = bf16[176,896]{1,0:T(8,128)(2,1)S(1)} collective-permute-done((bf16[176,896]{1,0:T(8,128)(2,1)}, bf16[176,896]{1,0:T(8,128)(2,1)S(1)}, u32[]{:S(2)}, u32[]{:S(2)}) %collective-permute-start.5) | collective-permute-done | bytes 315424 | tf_op jit(solution)/shard_map/cond/branch_1_fun/ppermute | solution.py:21
  39.8 4.6 %collective-permute-done.6.refs_1_ = bf16[176,896]{1,0:T(8,128)(2,1)S(1)} collective-permute-done((bf16[176,896]{1,0:T(8,128)(2,1)}, bf16[176,896]{1,0:T(8,128)(2,1)S(1)}, u32[]{:S(2)}, u32[]{:S(2)}) %collective-permute-start.6) | collective-permute-done | bytes 315424 | tf_op jit(solution)/shard_map/cond/branch_1_fun/ppermute | solution.py:21
  44.4 8.9 %collective-permute-done.7.refs_2_ = bf16[176,896]{1,0:T(8,128)(2,1)S(1)} collective-permute-done((bf16[176,896]{1,0:T(8,128)(2,1)}, bf16[176,896]{1,0:T(8,128)(2,1)S(1)}, u32[]{:S(2)}, u32[]{:S(2)}) %collective-permute-start.7) | collective-permute-done | bytes 315424 | tf_op jit(solution)/shard_map/cond/branch_1_fun/ppermute | solution.py:21
  53.3 1.0 pack.3.refs_1_
  54.3 2.3 %collective-permute-start.9 = (bf16[3,176,896]{2,1,0:T(8,128)(2,1)}, bf16[3,176,896]{2,1,0:T(8,128)(2,1)}, u32[]{:S(2)}, u32[]{:S(2)}) collective-permute-start(bf16[3,176,896]{2,1,0:T(8,128)(2,1)} %pack.3.refs_1_), channel_id=1, source_target_pairs={{0,1},{1,0},{2,3},{3,2},{4,5},{5,4},{6,7},{7,6},{8,9},{9,8},{10,11... | collective-permute-start | bytes 2838536 | tf_op jit(solution)/shard_map/cond/branch_1_fun/ppermute | solution.py:21
  56.6 0.0 copy-done.9
  56.6 2.0 %collective-permute-start.8 = (bf16[176,896]{1,0:T(8,128)(2,1)S(1)}, bf16[176,896]{1,0:T(8,128)(2,1)}, u32[]{:S(2)}, u32[]{:S(2)}) collective-permute-start(bf16[176,896]{1,0:T(8,128)(2,1)S(1)} %copy-done.9), channel_id=1, source_target_pairs={{0,1},{1,0},{2,3},{3,2},{4,5},{5,4},{6,7},{7,6},{8,9},{9,8},{10,11... | collective-permute-start | bytes 946184 | tf_op jit(solution)/shard_map/cond/branch_1_fun/ppermute | solution.py:21
  58.6 1.6 %collective-permute-done.8.refs_2_ = bf16[176,896]{1,0:T(8,128)(2,1)} collective-permute-done((bf16[176,896]{1,0:T(8,128)(2,1)S(1)}, bf16[176,896]{1,0:T(8,128)(2,1)}, u32[]{:S(2)}, u32[]{:S(2)}) %collective-permute-start.8) | collective-permute-done | bytes 315424 | tf_op jit(solution)/shard_map/cond/branch_1_fun/ppermute | solution.py:21
  60.3 0.0 collective-permute-done.9.refs_3_
  60.3 0.0 copy-done.6
  60.3 4.3 %forward.3 = bf16[16,88,512]{2,1,0:T(8,128)(2,1)} custom-call(bf16[176,896]{1,0:T(8,128)(2,1)S(1)} %copy-done.9, bf16[3,176,896]{2,1,0:T(8,128)(2,1)} %pack.3.refs_1_, bf16[176,896]{1,0:T(8,128)(2,1)} %collective-permute-done.8.refs_2_, bf16[3,176,896]{2,1,0:T(8,128)(2,1)} %collective-permute-done.9.refs_3_, bf16[896,512]{1,0:T(8,128)(2,1)S(1)} %copy-done.6), custom_call_target="tpu_custom_call" | custom-call | tf_op jit(solution)/shard_map/cond/branch_1_fun/forward/pallas_call | solution.py:85
  64.6 2.0 %all-to-all-done.1 = bf16[8,2,88,512]{3,2,1,0:T(8,128)(2,1)} async-done(((bf16[8,2,88,512]{3,2,1,0:T(8,128)(2,1)}), bf16[8,2,88,512]{3,2,1,0:T(8,128)(2,1)}, u32[]{:S(2)}, u32[]{:S(2)}) %all-to-all-start.1) | async-done | bytes 1441824 | tf_op jit(solution)/shard_map/cond/branch_1_fun/all_to_all | solution.py:25
  66.6 0.0 collective-permute-done.11.refs_7_
  66.7 0.0 collective-permute-done.12.refs_8_
  66.7 0.0 copy-start.3
  66.7 0.9 copy-done.3
  67.6 4.7 %all-to-all-start.2 = ((bf16[16,88,512]{2,1,0:T(8,128)(2,1)}), bf16[16,88,512]{2,1,0:T(8,128)(2,1)S(1)}, u32[]{:S(2)}, u32[]{:S(2)}) async-start(bf16[16,88,512]{2,1,0:T(8,128)(2,1)} %get-tuple-element.51), calls=%async_computation.2 | async-start | bytes 2883584 | tf_op jit(solution)/shard_map/all_to_all | solution.py:25
  72.3 0.0 copy-start.2
  72.3 0.0 copy-start.4
  72.3 0.0 copy-start.7
  72.3 5.6 %backward.1 = (bf16[4,176,896]{2,1,0:T(8,128)(2,1)}, bf16[4,176,896]{2,1,0:T(8,128)(2,1)}, bf16[8,176,512]{2,1,0:T(8,128)(2,1)}) custom-call(bf16[8,2,88,512]{3,2,1,0:T(8,128)(2,1)} %get-tuple-element.52.u, bf16[896,512]{1,0:T(8,128)(2,1)} %bitcast.19), custom_call_target="tpu_custom_call" | custom-call | tf_op jit(solution)/shard_map/backward/pallas_call | solution.py:108
  78.0 0.0 copy-start
  78.0 2.5 %collective-permute-start.13 = (bf16[4,176,896]{2,1,0:T(8,128)(2,1)}, bf16[4,176,896]{2,1,0:T(8,128)(2,1)S(1)}, u32[]{:S(2)}, u32[]{:S(2)}) collective-permute-start(bf16[4,176,896]{2,1,0:T(8,128)(2,1)} %get-tuple-element.53), channel_id=1, source_target_pairs={{0,1},{1,0},{2,3},{3,2},{4,5},{5,4},{6,7},{7,6},{8,9},{9,8},{10,11... | collective-permute-start | bytes 3784712 | tf_op jit(solution)/shard_map/ppermute | solution.py:21
  80.4 2.8 %collective-permute-done.13.got = bf16[4,176,896]{2,1,0:T(8,128)(2,1)S(1)} collective-permute-done((bf16[4,176,896]{2,1,0:T(8,128)(2,1)}, bf16[4,176,896]{2,1,0:T(8,128)(2,1)S(1)}, u32[]{:S(2)}, u32[]{:S(2)}) %collective-permute-start.13) | collective-permute-done | bytes 1261600 | tf_op jit(solution)/shard_map/ppermute | solution.py:21
  83.2 0.0 copy-start.1
  83.2 1.3 %copy-done.1 = bf16[4,176,896]{2,1,0:T(8,128)(2,1)S(1)} copy-done((bf16[4,176,896]{2,1,0:T(8,128)(2,1)S(1)}, bf16[4,176,896]{2,1,0:T(8,128)(2,1)}, u32[]{:S(2)}) %copy-start.1) | copy-done | bytes 1261592
  84.5 0.3 merge.1
  84.8 2.2 %collective-permute-start.14 = (bf16[176,896]{1,0:T(8,128)(2,1)S(1)}, bf16[176,896]{1,0:T(8,128)(2,1)S(1)}, u32[]{:S(2)}, u32[]{:S(2)}) collective-permute-start(bf16[176,896]{1,0:T(8,128)(2,1)S(1)} %get-tuple-element.56), channel_id=1, source_target_pairs={{0,2},{2,4},{4,6},{6,0},{1,3},{3,5},{5,7},{7,1},{8,10},{10,12},{12... | collective-permute-start | bytes 946184 | tf_op jit(solution)/shard_map/ppermute | solution.py:21
  87.0 4.4 %collective-permute-start.15 = (bf16[176,896]{1,0:T(8,128)(2,1)S(1)}, bf16[176,896]{1,0:T(8,128)(2,1)S(1)}, u32[]{:S(2)}, u32[]{:S(2)}) collective-permute-start(bf16[176,896]{1,0:T(8,128)(2,1)S(1)} %get-tuple-element.57), channel_id=1, source_target_pairs={{0,4},{2,6},{4,0},{6,2},{1,5},{3,7},{5,1},{7,3},{8,12},{10,14},{12... | collective-permute-start | bytes 946184 | tf_op jit(solution)/shard_map/ppermute | solution.py:21
  91.4 3.1 %collective-permute-start.16 = (bf16[176,896]{1,0:T(8,128)(2,1)S(1)}, bf16[176,896]{1,0:T(8,128)(2,1)S(1)}, u32[]{:S(2)}, u32[]{:S(2)}) collective-permute-start(bf16[176,896]{1,0:T(8,128)(2,1)S(1)} %get-tuple-element.58), channel_id=1, source_target_pairs={{0,6},{2,0},{4,2},{6,4},{1,7},{3,1},{5,3},{7,5},{8,14},{10,8},{12,... | collective-permute-start | bytes 946184 | tf_op jit(solution)/shard_map/ppermute | solution.py:21
  94.5 0.0 copy-done.2
  94.5 0.0 copy-done.4
  94.5 0.0 copy-done.7
  94.5 0.0 copy-done
  94.5 6.6 %step.1 = bf16[896,512]{1,0:T(8,128)(2,1)} custom-call(bf16[176,896]{1,0:T(8,128)(2,1)S(1)} %bitcast.22, bf16[3,176,896]{2,1,0:T(8,128)(2,1)} %get-tuple-element.59.refs_1_, bf16[176,896]{1,0:T(8,128)(2,1)} %get-tuple-element.60.refs_2_, bf16[3,176,896]{2,1,0:T(8,128)(2,1)} %get-tuple-element.61.refs_3_, bf16[1408,512]{1,0:T(8,128)(2,1)S(1)} %bitcast.15, ...), custom_call_target="tpu_custom_call" | custom-call | tf_op jit(solution)/shard_map/step/pallas_call | solution.py:147
  101.1 0.0 collective-permute-done.14
  101.1 2.3 %collective-permute-done.15 = bf16[176,896]{1,0:T(8,128)(2,1)S(1)} collective-permute-done((bf16[176,896]{1,0:T(8,128)(2,1)S(1)}, bf16[176,896]{1,0:T(8,128)(2,1)S(1)}, u32[]{:S(2)}, u32[]{:S(2)}) %collective-permute-start.15) | collective-permute-done | bytes 315424 | tf_op jit(solution)/shard_map/ppermute | solution.py:21
  103.4 2.1 %collective-permute-done.16 = bf16[176,896]{1,0:T(8,128)(2,1)S(1)} collective-permute-done((bf16[176,896]{1,0:T(8,128)(2,1)S(1)}, bf16[176,896]{1,0:T(8,128)(2,1)S(1)}, u32[]{:S(2)}, u32[]{:S(2)}) %collective-permute-start.16) | collective-permute-done | bytes 315424 | tf_op jit(solution)/shard_map/ppermute | solution.py:21
  105.5 0.9 fusion.1
  106.4 0.4 all-to-all-done.2.parts
  106.8 0.8 total.1
Async XLA Ops:
  0.6 6.7 %copy-start.10 = (bf16[1,88,512]{2,1,0:T(8,128)(2,1)S(1)}, bf16[1,88,512]{2,1,0:T(8,128)(2,1)}, u32[]{:S(2)}) copy-start(bf16[1,88,512]{2,1,0:T(8,128)(2,1)} %param.8) | copy-start | bytes 270340
  0.6 8.5 %collective-permute-start.10 = (bf16[88,512]{1,0:T(8,128)(2,1)}, bf16[88,512]{1,0:T(8,128)(2,1)S(1)}, u32[]{:S(2)}, u32[]{:S(2)}) collective-permute-start(bf16[88,512]{1,0:T(8,128)(2,1)} %bitcast.24), channel_id=1, source_target_pairs={{0,64},{64,0},{1,65},{65,1},{2,66},{66,2},{3,67},{67,3},{4,68},{68... | collective-permute-start | bytes 270344 | tf_op jit(solution)/shard_map/ppermute | solution.py:21
  9.2 57.5 %collective-permute-start.11 = (bf16[896,512]{1,0:T(8,128)(2,1)S(1)}, bf16[896,512]{1,0:T(8,128)(2,1)S(1)}, u32[]{:S(2)}, u32[]{:S(2)}) collective-permute-start(bf16[896,512]{1,0:T(8,128)(2,1)S(1)} %fusion.refs_5_), channel_id=1, source_target_pairs={{0,128},{128,256},{256,384},{384,0},{1,129},{129,257},{257,385},{3... | collective-permute-start | bytes 2752520 | tf_op jit(solution)/shard_map/ppermute | solution.py:21
  15.0 51.7 %collective-permute-start.12 = (bf16[896,512]{1,0:T(8,128)(2,1)S(1)}, bf16[896,512]{1,0:T(8,128)(2,1)S(1)}, u32[]{:S(2)}, u32[]{:S(2)}) collective-permute-start(bf16[896,512]{1,0:T(8,128)(2,1)S(1)} %fusion.refs_5_), channel_id=1, source_target_pairs={{0,384},{128,0},{256,128},{384,256},{1,385},{129,1},{257,129},{385... | collective-permute-start | bytes 2752520 | tf_op jit(solution)/shard_map/ppermute | solution.py:21
  22.1 44.5 %all-to-all-start.1 = ((bf16[8,2,88,512]{3,2,1,0:T(8,128)(2,1)}), bf16[8,2,88,512]{3,2,1,0:T(8,128)(2,1)}, u32[]{:S(2)}, u32[]{:S(2)}) async-start(bf16[8,2,88,512]{3,2,1,0:T(8,128)(2,1)} %fan.3), calls=%async_computation.1 | async-start | bytes 2883584 | tf_op jit(solution)/shard_map/cond/branch_1_fun/all_to_all | solution.py:25
  28.9 27.7 %copy-start.9 = (bf16[176,896]{1,0:T(8,128)(2,1)S(1)}, bf16[176,896]{1,0:T(8,128)(2,1)}, u32[]{:S(2)}) copy-start(bf16[176,896]{1,0:T(8,128)(2,1)} %get-tuple-element.20.refs_0_) | copy-start | bytes 946180 | tf_op jit(solution)/shard_map/cond
  28.9 31.4 %copy-start.6 = (bf16[896,512]{1,0:T(8,128)(2,1)S(1)}, bf16[896,512]{1,0:T(8,128)(2,1)}, u32[]{:S(2)}) copy-start(bf16[896,512]{1,0:T(8,128)(2,1)} %get-tuple-element.21.refs_4_) | copy-start | bytes 2752516 | tf_op jit(solution)/shard_map/cond
  28.9 10.8 %collective-permute-start.5 = (bf16[176,896]{1,0:T(8,128)(2,1)}, bf16[176,896]{1,0:T(8,128)(2,1)S(1)}, u32[]{:S(2)}, u32[]{:S(2)}) collective-permute-start(bf16[176,896]{1,0:T(8,128)(2,1)} %get-tuple-element.20.refs_0_), channel_id=1, source_target_pairs={{0,6},{2,0},{4,2},{6,4},{1,7},{3,1},{5,3},{7,5},{8,14},{10,8},{12,... | collective-permute-start | bytes 946184 | tf_op jit(solution)/shard_map/cond/branch_1_fun/ppermute | solution.py:21
  33.5 10.9 %collective-permute-start.6 = (bf16[176,896]{1,0:T(8,128)(2,1)}, bf16[176,896]{1,0:T(8,128)(2,1)S(1)}, u32[]{:S(2)}, u32[]{:S(2)}) collective-permute-start(bf16[176,896]{1,0:T(8,128)(2,1)} %get-tuple-element.20.refs_0_), channel_id=1, source_target_pairs={{0,4},{2,6},{4,0},{6,2},{1,5},{3,7},{5,1},{7,3},{8,12},{10,14},{12... | collective-permute-start | bytes 946184 | tf_op jit(solution)/shard_map/cond/branch_1_fun/ppermute | solution.py:21
  35.9 17.4 %collective-permute-start.7 = (bf16[176,896]{1,0:T(8,128)(2,1)}, bf16[176,896]{1,0:T(8,128)(2,1)S(1)}, u32[]{:S(2)}, u32[]{:S(2)}) collective-permute-start(bf16[176,896]{1,0:T(8,128)(2,1)} %get-tuple-element.20.refs_0_), channel_id=1, source_target_pairs={{0,2},{2,4},{4,6},{6,0},{1,3},{3,5},{5,7},{7,1},{8,10},{10,12},{12... | collective-permute-start | bytes 946184 | tf_op jit(solution)/shard_map/cond/branch_1_fun/ppermute | solution.py:21
  54.3 6.0 %collective-permute-start.9 = (bf16[3,176,896]{2,1,0:T(8,128)(2,1)}, bf16[3,176,896]{2,1,0:T(8,128)(2,1)}, u32[]{:S(2)}, u32[]{:S(2)}) collective-permute-start(bf16[3,176,896]{2,1,0:T(8,128)(2,1)} %pack.3.refs_1_), channel_id=1, source_target_pairs={{0,1},{1,0},{2,3},{3,2},{4,5},{5,4},{6,7},{7,6},{8,9},{9,8},{10,11... | collective-permute-start | bytes 2838536 | tf_op jit(solution)/shard_map/cond/branch_1_fun/ppermute | solution.py:21
  56.6 3.6 %collective-permute-start.8 = (bf16[176,896]{1,0:T(8,128)(2,1)S(1)}, bf16[176,896]{1,0:T(8,128)(2,1)}, u32[]{:S(2)}, u32[]{:S(2)}) collective-permute-start(bf16[176,896]{1,0:T(8,128)(2,1)S(1)} %copy-done.9), channel_id=1, source_target_pairs={{0,1},{1,0},{2,3},{3,2},{4,5},{5,4},{6,7},{7,6},{8,9},{9,8},{10,11... | collective-permute-start | bytes 946184 | tf_op jit(solution)/shard_map/cond/branch_1_fun/ppermute | solution.py:21
  66.7 0.9 copy-start.3
  67.6 39.2 %all-to-all-start.2 = ((bf16[16,88,512]{2,1,0:T(8,128)(2,1)}), bf16[16,88,512]{2,1,0:T(8,128)(2,1)S(1)}, u32[]{:S(2)}, u32[]{:S(2)}) async-start(bf16[16,88,512]{2,1,0:T(8,128)(2,1)} %get-tuple-element.51), calls=%async_computation.2 | async-start | bytes 2883584 | tf_op jit(solution)/shard_map/all_to_all | solution.py:25
  72.3 22.2 %copy-start.2 = (bf16[1,896,512]{2,1,0:T(8,128)(2,1)S(1)}, bf16[1,896,512]{2,1,0:T(8,128)(2,1)}, u32[]{:S(2)}) copy-start(bf16[1,896,512]{2,1,0:T(8,128)(2,1)} %param.11) | copy-start | bytes 2752516
  72.3 22.2 %copy-start.4 = (bf16[896,512]{1,0:T(8,128)(2,1)S(1)}, bf16[896,512]{1,0:T(8,128)(2,1)}, u32[]{:S(2)}) copy-start(bf16[896,512]{1,0:T(8,128)(2,1)} %copy-done.3) | copy-start | bytes 2752516
  72.3 22.2 %copy-start.7 = (bf16[1,176,896]{2,1,0:T(8,128)(2,1)S(1)}, bf16[1,176,896]{2,1,0:T(8,128)(2,1)}, u32[]{:S(2)}) copy-start(bf16[1,176,896]{2,1,0:T(8,128)(2,1)} %param.7) | copy-start | bytes 946180
  78.0 16.5 %copy-start = (bf16[8,176,512]{2,1,0:T(8,128)(2,1)S(1)}, bf16[8,176,512]{2,1,0:T(8,128)(2,1)}, u32[]{:S(2)}) copy-start(bf16[8,176,512]{2,1,0:T(8,128)(2,1)} %get-tuple-element.62) | copy-start | bytes 4325380
  78.0 5.2 %collective-permute-start.13 = (bf16[4,176,896]{2,1,0:T(8,128)(2,1)}, bf16[4,176,896]{2,1,0:T(8,128)(2,1)S(1)}, u32[]{:S(2)}, u32[]{:S(2)}) collective-permute-start(bf16[4,176,896]{2,1,0:T(8,128)(2,1)} %get-tuple-element.53), channel_id=1, source_target_pairs={{0,1},{1,0},{2,3},{3,2},{4,5},{5,4},{6,7},{7,6},{8,9},{9,8},{10,11... | collective-permute-start | bytes 3784712 | tf_op jit(solution)/shard_map/ppermute | solution.py:21
  83.2 1.3 %copy-start.1 = (bf16[4,176,896]{2,1,0:T(8,128)(2,1)S(1)}, bf16[4,176,896]{2,1,0:T(8,128)(2,1)}, u32[]{:S(2)}) copy-start(bf16[4,176,896]{2,1,0:T(8,128)(2,1)} %get-tuple-element.54.keep) | copy-start | bytes 3784708
  84.8 16.3 %collective-permute-start.14 = (bf16[176,896]{1,0:T(8,128)(2,1)S(1)}, bf16[176,896]{1,0:T(8,128)(2,1)S(1)}, u32[]{:S(2)}, u32[]{:S(2)}) collective-permute-start(bf16[176,896]{1,0:T(8,128)(2,1)S(1)} %get-tuple-element.56), channel_id=1, source_target_pairs={{0,2},{2,4},{4,6},{6,0},{1,3},{3,5},{5,7},{7,1},{8,10},{10,12},{12... | collective-permute-start | bytes 946184 | tf_op jit(solution)/shard_map/ppermute | solution.py:21
  87.0 16.4 %collective-permute-start.15 = (bf16[176,896]{1,0:T(8,128)(2,1)S(1)}, bf16[176,896]{1,0:T(8,128)(2,1)S(1)}, u32[]{:S(2)}, u32[]{:S(2)}) collective-permute-start(bf16[176,896]{1,0:T(8,128)(2,1)S(1)} %get-tuple-element.57), channel_id=1, source_target_pairs={{0,4},{2,6},{4,0},{6,2},{1,5},{3,7},{5,1},{7,3},{8,12},{10,14},{12... | collective-permute-start | bytes 946184 | tf_op jit(solution)/shard_map/ppermute | solution.py:21
  91.4 14.2 %collective-permute-start.16 = (bf16[176,896]{1,0:T(8,128)(2,1)S(1)}, bf16[176,896]{1,0:T(8,128)(2,1)S(1)}, u32[]{:S(2)}, u32[]{:S(2)}) collective-permute-start(bf16[176,896]{1,0:T(8,128)(2,1)S(1)} %get-tuple-element.58), channel_id=1, source_target_pairs={{0,6},{2,0},{4,2},{6,4},{1,7},{3,1},{5,3},{7,5},{8,14},{10,8},{12,... | collective-permute-start | bytes 946184 | tf_op jit(solution)/shard_map/ppermute | solution.py:21

commit v4 on v3

--- a/solution.py
+++ b/solution.py
@@ -107,7 +107,7 @@
     half = pltpu.HBM((N_X, 2 * rows, w.shape[0]), BF16)
     return pl.pallas_call(
         backward_kernel,
-        out_shape=[half, half, pltpu.HBM((2 * N_X, 2 * rows, feats), BF16)],
+        out_shape=[jax.ShapeDtypeStruct(half.shape, BF16), half, pltpu.HBM((2 * N_X, 2 * rows, feats), BF16)],
         compiler_params=PARAMS,
         name="backward",
     )(u, w)

time: 109 us -> 108 us (level)
  transfers between devices with their start and end apart: 14 -> 14, of which waited for: 9 -> 9; matrix products, arithmetic and copies ran while one was open for 3% -> 3% of each run, Pallas kernels for 18% -> 17%
where the time goes in v4:
time: 108 us
  starting transfers between devices  54.1 us (50%)
  waiting for transfers between devices  26.4 us (24%)
  Pallas kernels  19.6 us (18%)
  local copies, waits for them, and re-layouts  2.77 us (3%)
  other arithmetic  2.61 us (2%)
  between operations  2.09 us (2%)
    ppermute x12, starting transfers between devices, shifted(): lax.ppermute(array, axis, [(i, (i + by) % peers) for i in range(peers)])  42.5 us
    ppermute x12, waiting for transfers between devices, shifted(): lax.ppermute(array, axis, [(i, (i + by) % peers) for i in range(peers)])  23.4 us
    all_to_all x2, starting transfers between devices, exchanged(): return lax.all_to_all(parts, axis, 0, 0, tiled=False)  11.5 us
    pallas_call x1, Pallas kernels, local_step(): pl.pallas_call(step_kernel, grid=(units // 128,), out_shape=jax.ShapeDtyp...  6.62 us
    pallas_call x1, Pallas kernels, backward(): pl.pallas_call(backward_kernel, out_shape=[jax.ShapeDtypeStruct(half.shap...  5.29 us
    pallas_call x1, Pallas kernels, forward(): pl.pallas_call(forward_kernel, out_shape=pltpu.HBM((4 * N_X, rows, w.shap...  4.35 us
    all_to_all x2, waiting for transfers between devices, exchanged(): return lax.all_to_all(parts, axis, 0, 0, tiled=False)  2.97 us
    unnamed x14, local copies, waits for them, and re-layouts  2.24 us
  transfers between devices with their start and end apart: 14, of which 9 were waited for; matrix products, arithmetic and copies ran while one was open for 3% of the time, Pallas kernels for 17%

profile of v4, /device:TPU:1, one launch (start us, length us, event | category | flops | bytes accessed | tf_op | source)
XLA Modules:
  0.0 107.6 jit_solution(6785030563945212657)
XLA Ops:
  0.6 0.0 copy-start.10
  0.6 5.0 %collective-permute-start.10 = (bf16[88,512]{1,0:T(8,128)(2,1)}, bf16[88,512]{1,0:T(8,128)(2,1)S(1)}, u32[]{:S(2)}, u32[]{:S(2)}) collective-permute-start(bf16[88,512]{1,0:T(8,128)(2,1)} %bitcast.24), channel_id=1, source_target_pairs={{0,64},{64,0},{1,65},{65,1},{2,66},{66,2},{3,67},{67,3},{4,68},{68... | collective-permute-start | bytes 270344 | tf_op jit(solution)/shard_map/ppermute | solution.py:21
  5.6 1.7 %fusion.refs_5_ = bf16[896,512]{1,0:T(8,128)(2,1)S(1)} fusion(bf16[1,896,512]{2,1,0:T(8,128)(2,1)} %param.10, bf16[1,896,512]{2,1,0:T(8,128)(2,1)} %param.9), kind=kLoop, calls=%fused_computation.1 | loop fusion | flops 2293760 | bytes 2752512 | tf_op jit(solution)/shard_map/convert_element_type | solution.py:186
  7.3 0.0 copy-done.10
  7.4 0.5 slice.5
  9.2 0.0 collective-permute-done.10
  9.2 5.8 %collective-permute-start.11 = (bf16[896,512]{1,0:T(8,128)(2,1)S(1)}, bf16[896,512]{1,0:T(8,128)(2,1)S(1)}, u32[]{:S(2)}, u32[]{:S(2)}) collective-permute-start(bf16[896,512]{1,0:T(8,128)(2,1)S(1)} %fusion.refs_5_), channel_id=1, source_target_pairs={{0,128},{128,256},{256,384},{384,0},{1,129},{129,257},{257,385},{3... | collective-permute-start | bytes 2752520 | tf_op jit(solution)/shard_map/ppermute | solution.py:21
  15.0 5.9 %collective-permute-start.12 = (bf16[896,512]{1,0:T(8,128)(2,1)S(1)}, bf16[896,512]{1,0:T(8,128)(2,1)S(1)}, u32[]{:S(2)}, u32[]{:S(2)}) collective-permute-start(bf16[896,512]{1,0:T(8,128)(2,1)S(1)} %fusion.refs_5_), channel_id=1, source_target_pairs={{0,384},{128,0},{256,128},{384,256},{1,385},{129,1},{257,129},{385... | collective-permute-start | bytes 2752520 | tf_op jit(solution)/shard_map/ppermute | solution.py:21
  20.9 45.8 %conditional.1 = (bf16[16,88,512]{2,1,0:T(8,128)(2,1)}, bf16[8,2,88,512]{3,2,1,0:T(8,128)(2,1)}, bf16[3,176,896]{2,1,0:T(8,128)(2,1)}, bf16[176,896]{1,0:T(8,128)(2,1)}, bf16[3,176,896]{2,1,0:T(8,128)(2,1)}) conditional(s32[]{:T(128)} %convert_element_type.28, (bf16[176,896]{1,0:T(8,128)(2,1)}, bf16[896,512]{1,0:T(8,128)(2,1)}, ...), branch_computations={%region_0.0_spmd, %region_1.0_spmd} | conditional | bytes 18088264 | solution.py:191
  20.9 1.2 %fan.3 = bf16[8,2,88,512]{3,2,1,0:T(8,128)(2,1)} custom-call(bf16[88,512]{1,0:T(8,128)(2,1)S(1)} %get-tuple-element.22.u, bf16[88,512]{1,0:T(8,128)(2,1)S(1)} %get-tuple-element.23.u_z), custom_call_target="tpu_custom_call" | custom-call | tf_op jit(solution)/shard_map/cond/branch_1_fun/fan/pallas_call | solution.py:58
  22.1 6.8 %all-to-all-start.1 = ((bf16[8,2,88,512]{3,2,1,0:T(8,128)(2,1)}), bf16[8,2,88,512]{3,2,1,0:T(8,128)(2,1)}, u32[]{:S(2)}, u32[]{:S(2)}) async-start(bf16[8,2,88,512]{3,2,1,0:T(8,128)(2,1)} %fan.3), calls=%async_computation.1 | async-start | bytes 2883584 | tf_op jit(solution)/shard_map/cond/branch_1_fun/all_to_all | solution.py:25
  28.9 0.0 copy-start.9
  28.9 0.0 copy-start.6
  28.9 4.5 %collective-permute-start.5 = (bf16[176,896]{1,0:T(8,128)(2,1)}, bf16[176,896]{1,0:T(8,128)(2,1)S(1)}, u32[]{:S(2)}, u32[]{:S(2)}) collective-permute-start(bf16[176,896]{1,0:T(8,128)(2,1)} %get-tuple-element.20.refs_0_), channel_id=1, source_target_pairs={{0,6},{2,0},{4,2},{6,4},{1,7},{3,1},{5,3},{7,5},{8,14},{10,8},{12,... | collective-permute-start | bytes 946184 | tf_op jit(solution)/shard_map/cond/branch_1_fun/ppermute | solution.py:21
  33.5 2.4 %collective-permute-start.6 = (bf16[176,896]{1,0:T(8,128)(2,1)}, bf16[176,896]{1,0:T(8,128)(2,1)S(1)}, u32[]{:S(2)}, u32[]{:S(2)}) collective-permute-start(bf16[176,896]{1,0:T(8,128)(2,1)} %get-tuple-element.20.refs_0_), channel_id=1, source_target_pairs={{0,4},{2,6},{4,0},{6,2},{1,5},{3,7},{5,1},{7,3},{8,12},{10,14},{12... | collective-permute-start | bytes 946184 | tf_op jit(solution)/shard_map/cond/branch_1_fun/ppermute | solution.py:21
  35.9 2.5 %collective-permute-start.7 = (bf16[176,896]{1,0:T(8,128)(2,1)}, bf16[176,896]{1,0:T(8,128)(2,1)S(1)}, u32[]{:S(2)}, u32[]{:S(2)}) collective-permute-start(bf16[176,896]{1,0:T(8,128)(2,1)} %get-tuple-element.20.refs_0_), channel_id=1, source_target_pairs={{0,2},{2,4},{4,6},{6,0},{1,3},{3,5},{5,7},{7,1},{8,10},{10,12},{12... | collective-permute-start | bytes 946184 | tf_op jit(solution)/shard_map/cond/branch_1_fun/ppermute | solution.py:21
  38.4 1.3 %collective-permute-done.5.refs_0_ = bf16[176,896]{1,0:T(8,128)(2,1)S(1)} collective-permute-done((bf16[176,896]{1,0:T(8,128)(2,1)}, bf16[176,896]{1,0:T(8,128)(2,1)S(1)}, u32[]{:S(2)}, u32[]{:S(2)}) %collective-permute-start.5) | collective-permute-done | bytes 315424 | tf_op jit(solution)/shard_map/cond/branch_1_fun/ppermute | solution.py:21
  39.8 4.6 %collective-permute-done.6.refs_1_ = bf16[176,896]{1,0:T(8,128)(2,1)S(1)} collective-permute-done((bf16[176,896]{1,0:T(8,128)(2,1)}, bf16[176,896]{1,0:T(8,128)(2,1)S(1)}, u32[]{:S(2)}, u32[]{:S(2)}) %collective-permute-start.6) | collective-permute-done | bytes 315424 | tf_op jit(solution)/shard_map/cond/branch_1_fun/ppermute | solution.py:21
  44.4 8.9 %collective-permute-done.7.refs_2_ = bf16[176,896]{1,0:T(8,128)(2,1)S(1)} collective-permute-done((bf16[176,896]{1,0:T(8,128)(2,1)}, bf16[176,896]{1,0:T(8,128)(2,1)S(1)}, u32[]{:S(2)}, u32[]{:S(2)}) %collective-permute-start.7) | collective-permute-done | bytes 315424 | tf_op jit(solution)/shard_map/cond/branch_1_fun/ppermute | solution.py:21
  53.3 1.0 pack.3.refs_1_
  54.3 2.3 %collective-permute-start.9 = (bf16[3,176,896]{2,1,0:T(8,128)(2,1)}, bf16[3,176,896]{2,1,0:T(8,128)(2,1)}, u32[]{:S(2)}, u32[]{:S(2)}) collective-permute-start(bf16[3,176,896]{2,1,0:T(8,128)(2,1)} %pack.3.refs_1_), channel_id=1, source_target_pairs={{0,1},{1,0},{2,3},{3,2},{4,5},{5,4},{6,7},{7,6},{8,9},{9,8},{10,11... | collective-permute-start | bytes 2838536 | tf_op jit(solution)/shard_map/cond/branch_1_fun/ppermute | solution.py:21
  56.6 0.0 copy-done.9
  56.6 2.0 %collective-permute-start.8 = (bf16[176,896]{1,0:T(8,128)(2,1)S(1)}, bf16[176,896]{1,0:T(8,128)(2,1)}, u32[]{:S(2)}, u32[]{:S(2)}) collective-permute-start(bf16[176,896]{1,0:T(8,128)(2,1)S(1)} %copy-done.9), channel_id=1, source_target_pairs={{0,1},{1,0},{2,3},{3,2},{4,5},{5,4},{6,7},{7,6},{8,9},{9,8},{10,11... | collective-permute-start | bytes 946184 | tf_op jit(solution)/shard_map/cond/branch_1_fun/ppermute | solution.py:21
  58.6 1.6 %collective-permute-done.8.refs_2_ = bf16[176,896]{1,0:T(8,128)(2,1)} collective-permute-done((bf16[176,896]{1,0:T(8,128)(2,1)S(1)}, bf16[176,896]{1,0:T(8,128)(2,1)}, u32[]{:S(2)}, u32[]{:S(2)}) %collective-permute-start.8) | collective-permute-done | bytes 315424 | tf_op jit(solution)/shard_map/cond/branch_1_fun/ppermute | solution.py:21
  60.3 0.0 collective-permute-done.9.refs_3_
  60.3 0.0 copy-done.6
  60.3 4.3 %forward.3 = bf16[16,88,512]{2,1,0:T(8,128)(2,1)} custom-call(bf16[176,896]{1,0:T(8,128)(2,1)S(1)} %copy-done.9, bf16[3,176,896]{2,1,0:T(8,128)(2,1)} %pack.3.refs_1_, bf16[176,896]{1,0:T(8,128)(2,1)} %collective-permute-done.8.refs_2_, bf16[3,176,896]{2,1,0:T(8,128)(2,1)} %collective-permute-done.9.refs_3_, bf16[896,512]{1,0:T(8,128)(2,1)S(1)} %copy-done.6), custom_call_target="tpu_custom_call" | custom-call | tf_op jit(solution)/shard_map/cond/branch_1_fun/forward/pallas_call | solution.py:85
  64.6 2.0 %all-to-all-done.1 = bf16[8,2,88,512]{3,2,1,0:T(8,128)(2,1)} async-done(((bf16[8,2,88,512]{3,2,1,0:T(8,128)(2,1)}), bf16[8,2,88,512]{3,2,1,0:T(8,128)(2,1)}, u32[]{:S(2)}, u32[]{:S(2)}) %all-to-all-start.1) | async-done | bytes 1441824 | tf_op jit(solution)/shard_map/cond/branch_1_fun/all_to_all | solution.py:25
  66.6 0.0 collective-permute-done.11.refs_7_
  66.7 0.0 collective-permute-done.12.refs_8_
  66.7 0.0 copy-start.3
  66.7 0.9 copy-done.3
  67.6 4.7 %all-to-all-start.2 = ((bf16[16,88,512]{2,1,0:T(8,128)(2,1)}), bf16[16,88,512]{2,1,0:T(8,128)(2,1)S(1)}, u32[]{:S(2)}, u32[]{:S(2)}) async-start(bf16[16,88,512]{2,1,0:T(8,128)(2,1)} %get-tuple-element.51), calls=%async_computation.2 | async-start | bytes 2883584 | tf_op jit(solution)/shard_map/all_to_all | solution.py:25
  72.3 0.0 copy-start.2
  72.3 0.0 copy-start.4
  72.3 0.0 copy-start.7
  72.3 5.3 %backward.1 = (bf16[4,176,896]{2,1,0:T(8,128)(2,1)S(1)}, bf16[4,176,896]{2,1,0:T(8,128)(2,1)}, bf16[8,176,512]{2,1,0:T(8,128)(2,1)}) custom-call(bf16[8,2,88,512]{3,2,1,0:T(8,128)(2,1)} %get-tuple-element.52.u, bf16[896,512]{1,0:T(8,128)(2,1)} %bitcast.19), custom_call_target="tpu_custom_call" | custom-call | tf_op jit(solution)/shard_map/backward/pallas_call | solution.py:108
  77.6 0.0 copy-start
  77.6 2.5 %collective-permute-start.13 = (bf16[4,176,896]{2,1,0:T(8,128)(2,1)S(1)}, bf16[4,176,896]{2,1,0:T(8,128)(2,1)S(1)}, u32[]{:S(2)}, u32[]{:S(2)}) collective-permute-start(bf16[4,176,896]{2,1,0:T(8,128)(2,1)S(1)} %get-tuple-element.53), channel_id=1, source_target_pairs={{0,1},{1,0},{2,3},{3,2},{4,5},{5,4},{6,7},{7,6},{8,9},{9,8},{10,11... | collective-permute-start | bytes 3784712 | tf_op jit(solution)/shard_map/ppermute | solution.py:21
  80.1 2.6 %collective-permute-done.13.got = bf16[4,176,896]{2,1,0:T(8,128)(2,1)S(1)} collective-permute-done((bf16[4,176,896]{2,1,0:T(8,128)(2,1)S(1)}, bf16[4,176,896]{2,1,0:T(8,128)(2,1)S(1)}, u32[]{:S(2)}, u32[]{:S(2)}) %collective-permute-start.13) | collective-permute-done | bytes 1261600 | tf_op jit(solution)/shard_map/ppermute | solution.py:21
  82.7 0.0 copy-start.1
  82.7 1.3 %copy-done.1 = bf16[4,176,896]{2,1,0:T(8,128)(2,1)S(1)} copy-done((bf16[4,176,896]{2,1,0:T(8,128)(2,1)S(1)}, bf16[4,176,896]{2,1,0:T(8,128)(2,1)}, u32[]{:S(2)}) %copy-start.1) | copy-done | bytes 1261592
  84.0 0.3 merge.1
  84.2 2.2 %collective-permute-start.14 = (bf16[176,896]{1,0:T(8,128)(2,1)S(1)}, bf16[176,896]{1,0:T(8,128)(2,1)S(1)}, u32[]{:S(2)}, u32[]{:S(2)}) collective-permute-start(bf16[176,896]{1,0:T(8,128)(2,1)S(1)} %get-tuple-element.56), channel_id=1, source_target_pairs={{0,2},{2,4},{4,6},{6,0},{1,3},{3,5},{5,7},{7,1},{8,10},{10,12},{12... | collective-permute-start | bytes 946184 | tf_op jit(solution)/shard_map/ppermute | solution.py:21
  86.5 4.4 %collective-permute-start.15 = (bf16[176,896]{1,0:T(8,128)(2,1)S(1)}, bf16[176,896]{1,0:T(8,128)(2,1)S(1)}, u32[]{:S(2)}, u32[]{:S(2)}) collective-permute-start(bf16[176,896]{1,0:T(8,128)(2,1)S(1)} %get-tuple-element.57), channel_id=1, source_target_pairs={{0,4},{2,6},{4,0},{6,2},{1,5},{3,7},{5,1},{7,3},{8,12},{10,14},{12... | collective-permute-start | bytes 946184 | tf_op jit(solution)/shard_map/ppermute | solution.py:21
  90.8 3.1 %collective-permute-start.16 = (bf16[176,896]{1,0:T(8,128)(2,1)S(1)}, bf16[176,896]{1,0:T(8,128)(2,1)S(1)}, u32[]{:S(2)}, u32[]{:S(2)}) collective-permute-start(bf16[176,896]{1,0:T(8,128)(2,1)S(1)} %get-tuple-element.58), channel_id=1, source_target_pairs={{0,6},{2,0},{4,2},{6,4},{1,7},{3,1},{5,3},{7,5},{8,14},{10,8},{12,... | collective-permute-start | bytes 946184 | tf_op jit(solution)/shard_map/ppermute | solution.py:21
  93.9 0.0 copy-done.2
  93.9 0.0 copy-done.4
  93.9 0.0 copy-done.7
  94.0 0.0 copy-done
  94.0 6.6 %step.1 = bf16[896,512]{1,0:T(8,128)(2,1)} custom-call(bf16[176,896]{1,0:T(8,128)(2,1)S(1)} %bitcast.22, bf16[3,176,896]{2,1,0:T(8,128)(2,1)} %get-tuple-element.59.refs_1_, bf16[176,896]{1,0:T(8,128)(2,1)} %get-tuple-element.60.refs_2_, bf16[3,176,896]{2,1,0:T(8,128)(2,1)} %get-tuple-element.61.refs_3_, bf16[1408,512]{1,0:T(8,128)(2,1)S(1)} %bitcast.15, ...), custom_call_target="tpu_custom_call" | custom-call | tf_op jit(solution)/shard_map/step/pallas_call | solution.py:147
  100.6 0.0 collective-permute-done.14
  100.6 2.3 %collective-permute-done.15 = bf16[176,896]{1,0:T(8,128)(2,1)S(1)} collective-permute-done((bf16[176,896]{1,0:T(8,128)(2,1)S(1)}, bf16[176,896]{1,0:T(8,128)(2,1)S(1)}, u32[]{:S(2)}, u32[]{:S(2)}) %collective-permute-start.15) | collective-permute-done | bytes 315424 | tf_op jit(solution)/shard_map/ppermute | solution.py:21
  102.9 2.1 %collective-permute-done.16 = bf16[176,896]{1,0:T(8,128)(2,1)S(1)} collective-permute-done((bf16[176,896]{1,0:T(8,128)(2,1)S(1)}, bf16[176,896]{1,0:T(8,128)(2,1)S(1)}, u32[]{:S(2)}, u32[]{:S(2)}) %collective-permute-start.16) | collective-permute-done | bytes 315424 | tf_op jit(solution)/shard_map/ppermute | solution.py:21
  105.0 0.9 fusion.1
  105.9 0.9 all-to-all-done.2.parts
  106.8 0.8 total.1
Async XLA Ops:
  0.6 6.7 %copy-start.10 = (bf16[1,88,512]{2,1,0:T(8,128)(2,1)S(1)}, bf16[1,88,512]{2,1,0:T(8,128)(2,1)}, u32[]{:S(2)}) copy-start(bf16[1,88,512]{2,1,0:T(8,128)(2,1)} %param.8) | copy-start | bytes 270340
  0.6 8.5 %collective-permute-start.10 = (bf16[88,512]{1,0:T(8,128)(2,1)}, bf16[88,512]{1,0:T(8,128)(2,1)S(1)}, u32[]{:S(2)}, u32[]{:S(2)}) collective-permute-start(bf16[88,512]{1,0:T(8,128)(2,1)} %bitcast.24), channel_id=1, source_target_pairs={{0,64},{64,0},{1,65},{65,1},{2,66},{66,2},{3,67},{67,3},{4,68},{68... | collective-permute-start | bytes 270344 | tf_op jit(solution)/shard_map/ppermute | solution.py:21
  9.2 57.5 %collective-permute-start.11 = (bf16[896,512]{1,0:T(8,128)(2,1)S(1)}, bf16[896,512]{1,0:T(8,128)(2,1)S(1)}, u32[]{:S(2)}, u32[]{:S(2)}) collective-permute-start(bf16[896,512]{1,0:T(8,128)(2,1)S(1)} %fusion.refs_5_), channel_id=1, source_target_pairs={{0,128},{128,256},{256,384},{384,0},{1,129},{129,257},{257,385},{3... | collective-permute-start | bytes 2752520 | tf_op jit(solution)/shard_map/ppermute | solution.py:21
  15.0 51.7 %collective-permute-start.12 = (bf16[896,512]{1,0:T(8,128)(2,1)S(1)}, bf16[896,512]{1,0:T(8,128)(2,1)S(1)}, u32[]{:S(2)}, u32[]{:S(2)}) collective-permute-start(bf16[896,512]{1,0:T(8,128)(2,1)S(1)} %fusion.refs_5_), channel_id=1, source_target_pairs={{0,384},{128,0},{256,128},{384,256},{1,385},{129,1},{257,129},{385... | collective-permute-start | bytes 2752520 | tf_op jit(solution)/shard_map/ppermute | solution.py:21
  22.1 44.5 %all-to-all-start.1 = ((bf16[8,2,88,512]{3,2,1,0:T(8,128)(2,1)}), bf16[8,2,88,512]{3,2,1,0:T(8,128)(2,1)}, u32[]{:S(2)}, u32[]{:S(2)}) async-start(bf16[8,2,88,512]{3,2,1,0:T(8,128)(2,1)} %fan.3), calls=%async_computation.1 | async-start | bytes 2883584 | tf_op jit(solution)/shard_map/cond/branch_1_fun/all_to_all | solution.py:25
  28.9 27.7 %copy-start.9 = (bf16[176,896]{1,0:T(8,128)(2,1)S(1)}, bf16[176,896]{1,0:T(8,128)(2,1)}, u32[]{:S(2)}) copy-start(bf16[176,896]{1,0:T(8,128)(2,1)} %get-tuple-element.20.refs_0_) | copy-start | bytes 946180 | tf_op jit(solution)/shard_map/cond
  28.9 31.3 %copy-start.6 = (bf16[896,512]{1,0:T(8,128)(2,1)S(1)}, bf16[896,512]{1,0:T(8,128)(2,1)}, u32[]{:S(2)}) copy-start(bf16[896,512]{1,0:T(8,128)(2,1)} %get-tuple-element.21.refs_4_) | copy-start | bytes 2752516 | tf_op jit(solution)/shard_map/cond
  28.9 10.8 %collective-permute-start.5 = (bf16[176,896]{1,0:T(8,128)(2,1)}, bf16[176,896]{1,0:T(8,128)(2,1)S(1)}, u32[]{:S(2)}, u32[]{:S(2)}) collective-permute-start(bf16[176,896]{1,0:T(8,128)(2,1)} %get-tuple-element.20.refs_0_), channel_id=1, source_target_pairs={{0,6},{2,0},{4,2},{6,4},{1,7},{3,1},{5,3},{7,5},{8,14},{10,8},{12,... | collective-permute-start | bytes 946184 | tf_op jit(solution)/shard_map/cond/branch_1_fun/ppermute | solution.py:21
  33.5 10.9 %collective-permute-start.6 = (bf16[176,896]{1,0:T(8,128)(2,1)}, bf16[176,896]{1,0:T(8,128)(2,1)S(1)}, u32[]{:S(2)}, u32[]{:S(2)}) collective-permute-start(bf16[176,896]{1,0:T(8,128)(2,1)} %get-tuple-element.20.refs_0_), channel_id=1, source_target_pairs={{0,4},{2,6},{4,0},{6,2},{1,5},{3,7},{5,1},{7,3},{8,12},{10,14},{12... | collective-permute-start | bytes 946184 | tf_op jit(solution)/shard_map/cond/branch_1_fun/ppermute | solution.py:21
  35.9 17.4 %collective-permute-start.7 = (bf16[176,896]{1,0:T(8,128)(2,1)}, bf16[176,896]{1,0:T(8,128)(2,1)S(1)}, u32[]{:S(2)}, u32[]{:S(2)}) collective-permute-start(bf16[176,896]{1,0:T(8,128)(2,1)} %get-tuple-element.20.refs_0_), channel_id=1, source_target_pairs={{0,2},{2,4},{4,6},{6,0},{1,3},{3,5},{5,7},{7,1},{8,10},{10,12},{12... | collective-permute-start | bytes 946184 | tf_op jit(solution)/shard_map/cond/branch_1_fun/ppermute | solution.py:21
  54.3 6.0 %collective-permute-start.9 = (bf16[3,176,896]{2,1,0:T(8,128)(2,1)}, bf16[3,176,896]{2,1,0:T(8,128)(2,1)}, u32[]{:S(2)}, u32[]{:S(2)}) collective-permute-start(bf16[3,176,896]{2,1,0:T(8,128)(2,1)} %pack.3.refs_1_), channel_id=1, source_target_pairs={{0,1},{1,0},{2,3},{3,2},{4,5},{5,4},{6,7},{7,6},{8,9},{9,8},{10,11... | collective-permute-start | bytes 2838536 | tf_op jit(solution)/shard_map/cond/branch_1_fun/ppermute | solution.py:21
  56.6 3.6 %collective-permute-start.8 = (bf16[176,896]{1,0:T(8,128)(2,1)S(1)}, bf16[176,896]{1,0:T(8,128)(2,1)}, u32[]{:S(2)}, u32[]{:S(2)}) collective-permute-start(bf16[176,896]{1,0:T(8,128)(2,1)S(1)} %copy-done.9), channel_id=1, source_target_pairs={{0,1},{1,0},{2,3},{3,2},{4,5},{5,4},{6,7},{7,6},{8,9},{9,8},{10,11... | collective-permute-start | bytes 946184 | tf_op jit(solution)/shard_map/cond/branch_1_fun/ppermute | solution.py:21
  66.7 0.9 copy-start.3
  67.6 39.2 %all-to-all-start.2 = ((bf16[16,88,512]{2,1,0:T(8,128)(2,1)}), bf16[16,88,512]{2,1,0:T(8,128)(2,1)S(1)}, u32[]{:S(2)}, u32[]{:S(2)}) async-start(bf16[16,88,512]{2,1,0:T(8,128)(2,1)} %get-tuple-element.51), calls=%async_computation.2 | async-start | bytes 2883584 | tf_op jit(solution)/shard_map/all_to_all | solution.py:25
  72.3 21.6 %copy-start.2 = (bf16[1,896,512]{2,1,0:T(8,128)(2,1)S(1)}, bf16[1,896,512]{2,1,0:T(8,128)(2,1)}, u32[]{:S(2)}) copy-start(bf16[1,896,512]{2,1,0:T(8,128)(2,1)} %param.11) | copy-start | bytes 2752516
  72.3 21.6 %copy-start.4 = (bf16[896,512]{1,0:T(8,128)(2,1)S(1)}, bf16[896,512]{1,0:T(8,128)(2,1)}, u32[]{:S(2)}) copy-start(bf16[896,512]{1,0:T(8,128)(2,1)} %copy-done.3) | copy-start | bytes 2752516
  72.3 21.6 %copy-start.7 = (bf16[1,176,896]{2,1,0:T(8,128)(2,1)S(1)}, bf16[1,176,896]{2,1,0:T(8,128)(2,1)}, u32[]{:S(2)}) copy-start(bf16[1,176,896]{2,1,0:T(8,128)(2,1)} %param.7) | copy-start | bytes 946180
  77.6 16.3 %copy-start = (bf16[8,176,512]{2,1,0:T(8,128)(2,1)S(1)}, bf16[8,176,512]{2,1,0:T(8,128)(2,1)}, u32[]{:S(2)}) copy-start(bf16[8,176,512]{2,1,0:T(8,128)(2,1)} %get-tuple-element.62) | copy-start | bytes 4325380
  77.6 5.0 %collective-permute-start.13 = (bf16[4,176,896]{2,1,0:T(8,128)(2,1)S(1)}, bf16[4,176,896]{2,1,0:T(8,128)(2,1)S(1)}, u32[]{:S(2)}, u32[]{:S(2)}) collective-permute-start(bf16[4,176,896]{2,1,0:T(8,128)(2,1)S(1)} %get-tuple-element.53), channel_id=1, source_target_pairs={{0,1},{1,0},{2,3},{3,2},{4,5},{5,4},{6,7},{7,6},{8,9},{9,8},{10,11... | collective-permute-start | bytes 3784712 | tf_op jit(solution)/shard_map/ppermute | solution.py:21
  82.7 1.3 %copy-start.1 = (bf16[4,176,896]{2,1,0:T(8,128)(2,1)S(1)}, bf16[4,176,896]{2,1,0:T(8,128)(2,1)}, u32[]{:S(2)}) copy-start(bf16[4,176,896]{2,1,0:T(8,128)(2,1)} %get-tuple-element.54.keep) | copy-start | bytes 3784708
  84.2 16.4 %collective-permute-start.14 = (bf16[176,896]{1,0:T(8,128)(2,1)S(1)}, bf16[176,896]{1,0:T(8,128)(2,1)S(1)}, u32[]{:S(2)}, u32[]{:S(2)}) collective-permute-start(bf16[176,896]{1,0:T(8,128)(2,1)S(1)} %get-tuple-element.56), channel_id=1, source_target_pairs={{0,2},{2,4},{4,6},{6,0},{1,3},{3,5},{5,7},{7,1},{8,10},{10,12},{12... | collective-permute-start | bytes 946184 | tf_op jit(solution)/shard_map/ppermute | solution.py:21
  86.5 16.4 %collective-permute-start.15 = (bf16[176,896]{1,0:T(8,128)(2,1)S(1)}, bf16[176,896]{1,0:T(8,128)(2,1)S(1)}, u32[]{:S(2)}, u32[]{:S(2)}) collective-permute-start(bf16[176,896]{1,0:T(8,128)(2,1)S(1)} %get-tuple-element.57), channel_id=1, source_target_pairs={{0,4},{2,6},{4,0},{6,2},{1,5},{3,7},{5,1},{7,3},{8,12},{10,14},{12... | collective-permute-start | bytes 946184 | tf_op jit(solution)/shard_map/ppermute | solution.py:21
  90.8 14.1 %collective-permute-start.16 = (bf16[176,896]{1,0:T(8,128)(2,1)S(1)}, bf16[176,896]{1,0:T(8,128)(2,1)S(1)}, u32[]{:S(2)}, u32[]{:S(2)}) collective-permute-start(bf16[176,896]{1,0:T(8,128)(2,1)S(1)} %get-tuple-element.58), channel_id=1, source_target_pairs={{0,6},{2,0},{4,2},{6,4},{1,7},{3,1},{5,3},{7,5},{8,14},{10,8},{12,... | collective-permute-start | bytes 946184 | tf_op jit(solution)/shard_map/ppermute | solution.py:21
